TPU v7x, 128 devices: a whole 4x4x4 slice. The times are simulated.
128 devices in a mesh: band: 16 (over z, y_hi, core), comp: 8 (over x, y_lo).
Axes of the slice: x: 4, y: 4 (y_hi: 2, y_lo: 2; y = y_hi * 2 + y_lo), z: 4, core: 2. Of those that a mesh axis runs over, the one named last changes fastest.
Arguments:
- tracer_mass: float32 [192, 8, 256, 512], P('comp', None, 'band'), may hold values from -6 to 6
- layer_mass: float32 [8, 256, 512], P('comp', 'band'), may hold values from 0.3 to 1.7
- zonal_wind: float32 [8, 256, 512], P('comp', 'band'), may hold values from -4 to 4
- merid_wind: float32 [8, 256, 512], P('comp', 'band'), may hold values from -4 to 4
- group_counts: int32 [8], replicated, may hold values from 1 to 24, 96 in all
- limiter_flags: int32 [96], replicated, may hold values 0 or 1
Outputs:
- tracers_out: float32 [192, 8, 256, 512], P('comp', None, 'band')
- height_out: float32 [8, 256, 512], P('comp', 'band')
- zonal_out: float32 [8, 256, 512], P('comp', 'band')
- merid_out: float32 [8, 256, 512], P('comp', 'band')
Inputs may be any that keep to these rules, and one draw needn't show every extreme that they name: Group g lists the tracers numbered from the sum of the earlier groups' counts on, in its first group_counts[g] slots; the counts sum to 96 and the largest is exactly 24.
All inputs are finite; a program needn't handle non-finite values.
Results may differ from a plain program's by a relative error of at most 0.0003.
Values sent between devices are 32-bit elements; how exact they have to be, the bound alone decides.
A program may use at most 128 MiB of HBM per device.

v0:
```python
import functools

import jax
import jax.numpy as jnp
from jax import lax
from jax.experimental import pallas as pl
from jax.experimental.pallas import tpu as pltpu
from jax.sharding import PartitionSpec as P

STEPS = 4
CHUNK = 4
HALO = 8
ROWS = 16
EXT = ROWS + 2 * HALO
LEVELS = 8
NX = 512
SLOTS = 24
MESH_ID = pl.DeviceIdType.MESH
VMEM_LIMIT = 48 * 1024 * 1024

time_step = 0.1
gravity = 0.25
coriolis = 0.5
mass_floor = 0.5


def reach_of(step):
    return 2 * (STEPS - 1 - step)


def columns(i):
    return slice(128 * i, 128 * i + 128)


def level_rows(stage, first, stride):
    tiles = [
        stage[i, pl.ds(first, LEVELS, stride=stride), :] for i in range(NX // 128)
    ]
    return jnp.concatenate(tiles, axis=1)


def roll(value, shift):
    return pltpu.roll(value, shift % value.shape[-1], value.ndim - 1)


def gather_kernel(h_ref, u_ref, v_ref, out_ref, send_sem, recv_sem, halo_send, halo_recv):
    n_comp, n_band = lax.axis_size("comp"), lax.axis_size("band")
    level, band = lax.axis_index("comp"), lax.axis_index("band")
    has_low, has_high = band > 0, band < n_band - 1

    barrier = pltpu.get_barrier_semaphore()
    for p in range(1, n_comp):
        peer = lax.rem(level + p, n_comp)
        pl.semaphore_signal(barrier, inc=1, device_id={"comp": peer}, device_id_type=MESH_ID)

    @pl.when(has_low)
    def _():
        pl.semaphore_signal(barrier, inc=1, device_id={"band": band - 1}, device_id_type=MESH_ID)

    @pl.when(has_high)
    def _():
        pl.semaphore_signal(barrier, inc=1, device_id={"band": band + 1}, device_id_type=MESH_ID)

    for f, ref in enumerate((h_ref, u_ref, v_ref)):
        out_ref[level, f, HALO : HALO + ROWS, :] = ref[...]

    @pl.when(jnp.logical_not(has_low))
    def _():
        out_ref[level, :, 0:HALO, :] = jnp.zeros((3, HALO, NX), jnp.float32)

    @pl.when(jnp.logical_not(has_high))
    def _():
        out_ref[level, :, HALO + ROWS : EXT, :] = jnp.zeros((3, HALO, NX), jnp.float32)

    pl.semaphore_wait(
        barrier, n_comp - 1 + has_low.astype(jnp.int32) + has_high.astype(jnp.int32)
    )

    down = pltpu.make_async_remote_copy(
        src_ref=out_ref.at[level, :, pl.ds(HALO, HALO), :],
        dst_ref=out_ref.at[level, :, pl.ds(HALO + ROWS, HALO), :],
        send_sem=halo_send.at[0],
        recv_sem=halo_recv.at[0],
        device_id={"band": lax.max(band - 1, 0)},
        device_id_type=MESH_ID,
    )
    up = pltpu.make_async_remote_copy(
        src_ref=out_ref.at[level, :, pl.ds(ROWS, HALO), :],
        dst_ref=out_ref.at[level, :, pl.ds(0, HALO), :],
        send_sem=halo_send.at[1],
        recv_sem=halo_recv.at[1],
        device_id={"band": lax.min(band + 1, n_band - 1)},
        device_id_type=MESH_ID,
    )

    @pl.when(has_low)
    def _():
        down.start()

    @pl.when(has_high)
    def _():
        up.start()

    pieces = ((HALO, ROWS), (0, HALO), (HALO + ROWS, HALO))

    def copy(piece, p, owner):
        first, count = pieces[piece]
        return pltpu.make_async_remote_copy(
            src_ref=out_ref.at[owner, :, pl.ds(first, count), :],
            dst_ref=out_ref.at[owner, :, pl.ds(first, count), :],
            send_sem=send_sem.at[piece, p],
            recv_sem=recv_sem.at[piece, p],
            device_id={"comp": lax.rem(level + p, n_comp)},
            device_id_type=MESH_ID,
        )

    for p in range(1, n_comp):
        copy(0, p, level).start()

    @pl.when(has_low)
    def _():
        up.wait_recv()

    for p in range(1, n_comp):
        copy(1, p, level).start()

    @pl.when(has_high)
    def _():
        down.wait_recv()

    for p in range(1, n_comp):
        copy(2, p, level).start()

    @pl.when(has_low)
    def _():
        down.wait_send()

    @pl.when(has_high)
    def _():
        up.wait_send()

    for piece in range(3):
        for p in range(1, n_comp):
            copy(piece, p, level).wait_send()
            copy(piece, p, lax.rem(level + n_comp - p, n_comp)).wait_recv()


def gather_fields(height, zonal, merid):
    n_comp = lax.axis_size("comp")
    return pl.pallas_call(
        gather_kernel,
        out_shape=jax.ShapeDtypeStruct((n_comp, 3, EXT, NX), jnp.float32),
        in_specs=[pl.BlockSpec(memory_space=pltpu.VMEM)] * 3,
        out_specs=pl.BlockSpec(memory_space=pltpu.VMEM),
        scratch_shapes=[
            pltpu.SemaphoreType.DMA((3, n_comp)),
            pltpu.SemaphoreType.DMA((3, n_comp)),
            pltpu.SemaphoreType.DMA((2,)),
            pltpu.SemaphoreType.DMA((2,)),
        ],
        compiler_params=pltpu.CompilerParams(
            collective_id=0, has_side_effects=True, vmem_limit_bytes=16 * 1024 * 1024
        ),
    )(height, zonal, merid)


def dynamics_kernel(where_ref, g_ref, inv_ref, east_ref, south_ref, last_ref, h_buf, u_buf, v_buf, stage):
    first_row, level, total_rows = where_ref[0], where_ref[1], where_ref[2]
    stride = 3 * EXT

    for i in range(NX // 128):
        stage[i] = g_ref[:, columns(i)]

    @pl.loop(0, EXT)
    def _(j):
        for f, buf in enumerate((h_buf, u_buf, v_buf)):
            buf[j] = level_rows(stage, f * EXT + j, stride)

    depth = lax.broadcasted_iota(jnp.int32, (LEVELS, NX), 0)

    def geopot(h):
        total = h
        for gap in (1, 2, 4):
            moved = pltpu.roll(total, LEVELS - gap, 0)
            total = total + jnp.where(depth < LEVELS - gap, moved, 0.0)
        return gravity * total

    def south_flux(h_a, h_b, v_a, v_b, face):
        at = first_row + face - HALO
        inside = jnp.logical_and(at > 0, at < total_rows)
        scale = jnp.where(inside, 0.25 * time_step, 0.0)
        return scale * ((v_a + v_b) * (h_a + h_b))

    for step in range(STEPS):
        reach = reach_of(step)
        low, high = HALO - reach, HALO + ROWS + reach
        for j in (low - 2, low - 1, high, high + 1):
            inv_ref[step, j] = 1.0 / jnp.maximum(h_buf[j], mass_floor)
        h_before, h_here = h_buf[low - 1], h_buf[low]
        v_before, v_here = v_buf[low - 1], v_buf[low]
        south = south_flux(h_before, h_here, v_before, v_here, low)
        south_ref[step, low] = south

        def row(j, carry, step=step):
            h, v, geo_before, geo, south = carry
            h_after, v_after, u = h_buf[j + 1], v_buf[j + 1], u_buf[j]
            geo_after = geopot(h_after)
            south_after = south_flux(h, h_after, v, v_after, j + 1)
            east = (0.25 * time_step) * ((u + roll(u, -1)) * (h + roll(h, -1)))
            inv_ref[step, j] = 1.0 / jnp.maximum(h, mass_floor)
            east_ref[step, j] = east
            south_ref[step, j + 1] = south_after
            h_buf[j] = h - ((east - roll(east, 1)) + (south_after - south))
            u_buf[j] = u + time_step * (coriolis * v - 0.5 * (roll(geo, -1) - roll(geo, 1)))
            v_buf[j] = v - time_step * (coriolis * u + 0.5 * (geo_after - geo_before))
            return h_after, v_after, geo, geo_after, south_after

        lax.fori_loop(
            low, high, row, (h_here, v_here, geopot(h_before), geopot(h_here), south)
        )

    own = lax.broadcasted_iota(jnp.int32, (LEVELS, NX), 0) == level
    for f, buf in enumerate((h_buf, u_buf, v_buf)):
        for j in range(ROWS):
            picked = jnp.where(own, buf[HALO + j], 0.0)
            last_ref[f, pl.ds(j, 1), :] = jnp.sum(picked, axis=0, keepdims=True)


def dynamics(where, gathered):
    rows = jax.ShapeDtypeStruct((STEPS, EXT, LEVELS, NX), jnp.float32)
    vmem = pl.BlockSpec(memory_space=pltpu.VMEM)
    return pl.pallas_call(
        dynamics_kernel,
        out_shape=(rows, rows, rows, jax.ShapeDtypeStruct((3, ROWS, NX), jnp.float32)),
        in_specs=[pl.BlockSpec(memory_space=pltpu.SMEM), vmem],
        out_specs=(vmem,) * 4,
        scratch_shapes=[pltpu.VMEM((EXT, LEVELS, NX), jnp.float32)] * 3
        + [pltpu.VMEM((NX // 128, LEVELS * 3 * EXT, 128), jnp.float32)],
        compiler_params=pltpu.CompilerParams(vmem_limit_bytes=VMEM_LIMIT),
        cost_estimate=pl.CostEstimate(
            flops=10_000_000, bytes_accessed=8_000_000, transcendentals=0
        ),
    )(where, gathered)


def tracer_kernel(base, table_ref, m_ref, low_ref, high_ref, inv_ref, east_ref, south_ref, *rest):
    out_ref, buf, stage, low_stage, high_stage = rest[-5:]
    slot = base + pl.program_id(0)
    live = slot < table_ref[0]
    limited = table_ref[1 + slot] > 0

    def face(a_out, a, b, b_out, bounded):
        raw = (7.0 / 12.0) * (a + b) - (1.0 / 12.0) * (a_out + b_out)
        if not bounded:
            return raw
        return jnp.maximum(jnp.minimum(raw, jnp.maximum(a, b)), jnp.minimum(a, b))

    def advance(bounded):
        for step in range(STEPS):
            reach = reach_of(step)
            low, high = HALO - reach, HALO + ROWS + reach

            def ratio(j, step=step):
                return buf[j] * inv_ref[step, j]

            def row(j, carry, step=step):
                before, here, after, south = carry
                beyond = ratio(j + 2)
                south_after = south_ref[step, j + 1] * face(before, here, after, beyond, bounded)
                east = east_ref[step, j] * face(
                    roll(here, 1), here, roll(here, -1), roll(here, -2), bounded
                )
                new = buf[j] - ((east - roll(east, 1)) + (south_after - south))
                if step < STEPS - 1:
                    buf[j] = new
                else:
                    for i in range(NX // 128):
                        stage[i, pl.ds(j - HALO, LEVELS, stride=ROWS), :] = new[:, columns(i)]
                return here, after, beyond, south_after

            def rows(i, carry):
                for k in range(4):
                    carry = row(low + i * 4 + k, carry)
                return carry

            start = [ratio(low + k) for k in (-2, -1, 0, 1)]
            south = south_ref[step, low] * face(*start, bounded)
            lax.fori_loop(0, (high - low) // 4, rows, (*start[1:], south))

    @pl.when(live)
    def _():
        for i in range(NX // 128):
            stage[i] = m_ref[0, :, columns(i)]
            low_stage[i] = low_ref[0, :, columns(i)]
            high_stage[i] = high_ref[0, :, columns(i)]
        for j in range(HALO):
            buf[j] = level_rows(low_stage, j, HALO)
            buf[HALO + ROWS + j] = level_rows(high_stage, j, HALO)
        for j in range(ROWS):
            buf[HALO + j] = level_rows(stage, j, ROWS)

        @pl.when(limited)
        def _():
            advance(True)

        @pl.when(jnp.logical_not(limited))
        def _():
            advance(False)

        for i in range(NX // 128):
            out_ref[0, :, columns(i)] = stage[i]

    @pl.when(jnp.logical_not(live))
    def _():
        out_ref[...] = jnp.zeros_like(out_ref)


def tracer_chunk(base, count, table, mass, low, high, fluxes, so_far):
    slots = mass.shape[0]
    whole = pl.BlockSpec((STEPS, EXT, LEVELS, NX), lambda i, t: (0, 0, 0, 0), pipeline_mode=pl.Buffered(1))
    block = pl.BlockSpec((1, LEVELS * ROWS, NX), lambda i, t: (base + i, 0, 0))
    side = pl.BlockSpec((1, LEVELS * HALO, NX), lambda i, t: (i, 0, 0))
    operands = [table, mass, low, high, *fluxes]
    specs = [block, side, side, whole, whole, whole]
    aliases = {}
    if so_far is not None:
        aliases = {len(operands): 0}
        operands.append(so_far)
        specs.append(pl.BlockSpec(memory_space=pl.ANY))
    return pl.pallas_call(
        functools.partial(tracer_kernel, base),
        grid_spec=pltpu.PrefetchScalarGridSpec(
            num_scalar_prefetch=1,
            grid=(count,),
            in_specs=specs,
            out_specs=block,
            scratch_shapes=[
                pltpu.VMEM((EXT, LEVELS, NX), jnp.float32),
                pltpu.VMEM((NX // 128, LEVELS * ROWS, 128), jnp.float32),
                pltpu.VMEM((NX // 128, LEVELS * HALO, 128), jnp.float32),
                pltpu.VMEM((NX // 128, LEVELS * HALO, 128), jnp.float32),
            ],
        ),
        out_shape=jax.ShapeDtypeStruct((slots, LEVELS * ROWS, NX), jnp.float32),
        input_output_aliases=aliases,
        compiler_params=pltpu.CompilerParams(vmem_limit_bytes=VMEM_LIMIT),
        cost_estimate=pl.CostEstimate(
            flops=count * 11_000_000, bytes_accessed=6_000_000 + count * 800_000, transcendentals=0
        ),
    )(*operands)


def on_device(tracer_mass, layer_mass, zonal_wind, merid_wind, group_counts, limiter_flags):
    n_comp, n_band = lax.axis_size("comp"), lax.axis_size("band")
    comp, band = lax.axis_index("comp"), lax.axis_index("band")
    slots = tracer_mass.shape[0]

    groups = lax.broadcasted_iota(jnp.int32, (n_comp,), 0)
    count = jnp.sum(jnp.where(groups == comp, group_counts, 0))
    start = jnp.sum(jnp.where(groups < comp, group_counts, 0))
    numbers = lax.broadcasted_iota(jnp.int32, (slots, limiter_flags.shape[0]), 1)
    wanted = start + lax.broadcasted_iota(jnp.int32, (slots, limiter_flags.shape[0]), 0)
    flags = jnp.sum(jnp.where(numbers == wanted, limiter_flags[None, :], 0), 1)
    table = jnp.concatenate([count[None], flags])
    where = jnp.stack([band * ROWS, comp, n_band * ROWS]).astype(jnp.int32)

    forward = [(i, i + 1) for i in range(n_band - 1)]
    backward = [(i + 1, i) for i in range(n_band - 1)]

    gathered = gather_fields(
        layer_mass.reshape(ROWS, NX), zonal_wind.reshape(ROWS, NX), merid_wind.reshape(ROWS, NX)
    )
    lows, highs = [], []
    for base in range(0, slots, CHUNK):
        part = tracer_mass[base : base + CHUNK]
        lows.append(lax.ppermute(part[:, :, ROWS - HALO :], "band", forward))
        highs.append(lax.ppermute(part[:, :, :HALO], "band", backward))

    *fluxes, last = dynamics(where, gathered.reshape(n_comp * 3 * EXT, NX))
    mass = tracer_mass.reshape(slots, LEVELS * ROWS, NX)
    out = None
    for k, base in enumerate(range(0, slots, CHUNK)):
        low = lows[k].reshape(CHUNK, LEVELS * HALO, NX)
        high = highs[k].reshape(CHUNK, LEVELS * HALO, NX)
        out = tracer_chunk(base, CHUNK, table, mass, low, high, fluxes, out)
    tracers = out.reshape(tracer_mass.shape)
    return tracers, last[0][None], last[1][None], last[2][None]


def solution(mesh):
    placed = (
        P("comp", None, "band", None),
        P("comp", "band", None),
        P("comp", "band", None),
        P("comp", "band", None),
        P(),
        P(),
    )
    return jax.shard_map(
        on_device,
        mesh=mesh,
        in_specs=placed,
        out_specs=placed[:4],
        check_vma=False,
    )
```

profile of v0, /device:TPU:42, one launch (start us, length us, event | category | flops | bytes accessed | tf_op | source)
XLA Modules:
  0.0 250.8 jit_solution(18059079971231474972)
XLA Ops:
  0.7 5.2 %fusion.2 = (f32[4,8,8,512]{3,2,1,0:T(8,128)S(1)}, f32[4,8,8,512]{3,2,1,0:T(8,128)S(1)}, f32[4,8,8,512]{3,2,1,0:T(8,128)}, f32[4,8,8,512]{3,2,1,0:T(8,128)}, f32...) fusion(f32[24,8,16,512]{3,2,1,0:T(8,128)} %param.6), kind=kLoop, calls=%fused_computation.9 | loop fusion | bytes 12582912 | tf_op jit(solution)/shard_map/slice | solution.py:377
  5.9 3.2 %collective-permute-start.11 = (f32[4,8,8,512]{3,2,1,0:T(8,128)S(1)}, f32[4,8,8,512]{3,2,1,0:T(8,128)S(1)}, u32[]{:S(2)}, u32[]{:S(2)}) collective-permute-start(f32[4,8,8,512]{3,2,1,0:T(8,128)S(1)} %get-tuple-element.14), channel_id=1, source_target_pairs={{8,0},{16,8},{24,16},{32,24},{40,32},{48,40},{56,48},{64,56},{72,6... | collective-permute-start | bytes 1572872 | tf_op jit(solution)/shard_map/ppermute | solution.py:377
  9.1 2.6 %collective-permute-start.9 = (f32[4,8,8,512]{3,2,1,0:T(8,128)S(1)}, f32[4,8,8,512]{3,2,1,0:T(8,128)S(1)}, u32[]{:S(2)}, u32[]{:S(2)}) collective-permute-start(f32[4,8,8,512]{3,2,1,0:T(8,128)S(1)} %get-tuple-element.15), channel_id=1, source_target_pairs={{8,0},{16,8},{24,16},{32,24},{40,32},{48,40},{56,48},{64,56},{72,6... | collective-permute-start | bytes 1572872 | tf_op jit(solution)/shard_map/ppermute | solution.py:377
  11.7 1.9 collective-permute-start.8
  13.6 6.0 %collective-permute-start.7 = (f32[4,8,8,512]{3,2,1,0:T(8,128)}, f32[4,8,8,512]{3,2,1,0:T(8,128)S(1)}, u32[]{:S(2)}, u32[]{:S(2)}) collective-permute-start(f32[4,8,8,512]{3,2,1,0:T(8,128)} %get-tuple-element.17), channel_id=1, source_target_pairs={{8,0},{16,8},{24,16},{32,24},{40,32},{48,40},{56,48},{64,56},{72,6... | collective-permute-start | bytes 1572872 | tf_op jit(solution)/shard_map/ppermute | solution.py:377
  19.7 1.9 collective-permute-start.6
  21.6 6.0 %collective-permute-start.5 = (f32[4,8,8,512]{3,2,1,0:T(8,128)}, f32[4,8,8,512]{3,2,1,0:T(8,128)S(1)}, u32[]{:S(2)}, u32[]{:S(2)}) collective-permute-start(f32[4,8,8,512]{3,2,1,0:T(8,128)} %get-tuple-element.19), channel_id=1, source_target_pairs={{8,0},{16,8},{24,16},{32,24},{40,32},{48,40},{56,48},{64,56},{72,6... | collective-permute-start | bytes 1572872 | tf_op jit(solution)/shard_map/ppermute | solution.py:377
  27.7 1.9 collective-permute-start.10
  30.9 1.9 collective-permute-start.4
  32.8 5.2 %collective-permute-done.7 = f32[4,8,8,512]{3,2,1,0:T(8,128)S(1)} collective-permute-done((f32[4,8,8,512]{3,2,1,0:T(8,128)}, f32[4,8,8,512]{3,2,1,0:T(8,128)S(1)}, u32[]{:S(2)}, u32[]{:S(2)}) %collective-permute-start.7) | collective-permute-done | bytes 524320 | tf_op jit(solution)/shard_map/ppermute | solution.py:377
  38.1 6.1 %collective-permute-start.3 = (f32[4,8,8,512]{3,2,1,0:T(8,128)}, f32[4,8,8,512]{3,2,1,0:T(8,128)S(1)}, u32[]{:S(2)}, u32[]{:S(2)}) collective-permute-start(f32[4,8,8,512]{3,2,1,0:T(8,128)} %get-tuple-element.21), channel_id=1, source_target_pairs={{8,0},{16,8},{24,16},{32,24},{40,32},{48,40},{56,48},{64,56},{72,6... | collective-permute-start | bytes 1572872 | tf_op jit(solution)/shard_map/ppermute | solution.py:377
  44.2 1.9 collective-permute-start.2
  46.1 3.2 %collective-permute-done.5 = f32[4,8,8,512]{3,2,1,0:T(8,128)S(1)} collective-permute-done((f32[4,8,8,512]{3,2,1,0:T(8,128)}, f32[4,8,8,512]{3,2,1,0:T(8,128)S(1)}, u32[]{:S(2)}, u32[]{:S(2)}) %collective-permute-start.5) | collective-permute-done | bytes 524320 | tf_op jit(solution)/shard_map/ppermute | solution.py:377
  49.3 6.1 %collective-permute-start.1 = (f32[4,8,8,512]{3,2,1,0:T(8,128)}, f32[4,8,8,512]{3,2,1,0:T(8,128)S(1)}, u32[]{:S(2)}, u32[]{:S(2)}) collective-permute-start(f32[4,8,8,512]{3,2,1,0:T(8,128)} %get-tuple-element.23), channel_id=1, source_target_pairs={{8,0},{16,8},{24,16},{32,24},{40,32},{48,40},{56,48},{64,56},{72,6... | collective-permute-start | bytes 1572872 | tf_op jit(solution)/shard_map/ppermute | solution.py:377
  55.4 1.9 collective-permute-start
  57.4 45.5 %shard_map.93 = f32[8,3,32,512]{3,2,1,0:T(8,128)S(1)} custom-call(f32[16,512]{1,0:T(8,128)S(1)} %bitcast.33, f32[16,512]{1,0:T(8,128)S(1)} %bitcast.34, f32[16,512]{1,0:T(8,128)S(1)} %bitcast.35), custom_call_target="tpu_custom_call" | custom-call | tf_op jit(solution)/shard_map/pallas_call | solution.py:150
  102.9 17.3 %shard_map.94 = (f32[4,32,8,512]{3,2,1,0:T(8,128)S(1)}, f32[4,32,8,512]{3,2,1,0:T(8,128)S(1)}, f32[4,32,8,512]{3,2,1,0:T(8,128)}, f32[3,16,512]{2,1,0:T(8,128)S(1)}) custom-call(s32[3]{0:T(128)S(1)} %pad_add_fusion.1.where_ref, f32[768,512]{1,0:T(8,128)S(1)} %bitcast.21), custom_call_target="tpu_custom_call" | custom-call | flops 10000000 | bytes 8000000 | tf_op jit(solution)/shard_map/pallas_call | solution.py:232
  120.3 0.7 pad_add_fusion.table_ref
  121.7 21.6 %shard_map.95.rest_0_ = f32[24,128,512]{2,1,0:T(8,128)} custom-call(s32[25]{0:T(128)S(1)} %pad_add_fusion.table_ref, f32[24,128,512]{2,1,0:T(8,128)} %bitcast.36, f32[4,64,512]{2,1,0:T(8,128)} %bitcast.18.low_ref, f32[4,64,512]{2,1,0:T(8,128)S(1)} %bitcast.22, f32[4,32,8,512]{3,2,1,0:T(8,128)S(1)} %get-tuple-element.8.inv_ref, ...), custom_call_target="tpu_custom_call" | custom-call | flops 44000000 | bytes 9200000 | tf_op jit(solution)/shard_map/pallas_call | solution.py:330
  143.3 21.5 %shard_map.96.rest_0_ = f32[24,128,512]{2,1,0:T(8,128)} custom-call(s32[25]{0:T(128)S(1)} %pad_add_fusion.table_ref, f32[24,128,512]{2,1,0:T(8,128)} %bitcast.37, f32[4,64,512]{2,1,0:T(8,128)S(1)} %bitcast.24, f32[4,64,512]{2,1,0:T(8,128)S(1)} %bitcast.23, f32[4,32,8,512]{3,2,1,0:T(8,128)S(1)} %get-tuple-element.8.inv_ref, ...), custom_call_target="tpu_custom_call", output_to_operand_aliasing={{}: (7, {})} | custom-call | flops 44000000 | bytes 9200000 | tf_op jit(solution)/shard_map/pallas_call | solution.py:330
  164.8 21.5 %shard_map.97.rest_0_ = f32[24,128,512]{2,1,0:T(8,128)} custom-call(s32[25]{0:T(128)S(1)} %pad_add_fusion.table_ref, f32[24,128,512]{2,1,0:T(8,128)} %bitcast.38, f32[4,64,512]{2,1,0:T(8,128)S(1)} %bitcast.26, f32[4,64,512]{2,1,0:T(8,128)S(1)} %bitcast.25, f32[4,32,8,512]{3,2,1,0:T(8,128)S(1)} %get-tuple-element.8.inv_ref, ...), custom_call_target="tpu_custom_call", output_to_operand_aliasing={{}: (7, {})} | custom-call | flops 44000000 | bytes 9200000 | tf_op jit(solution)/shard_map/pallas_call | solution.py:330
  186.3 21.5 %shard_map.98.rest_0_ = f32[24,128,512]{2,1,0:T(8,128)} custom-call(s32[25]{0:T(128)S(1)} %pad_add_fusion.table_ref, f32[24,128,512]{2,1,0:T(8,128)} %bitcast.39, f32[4,64,512]{2,1,0:T(8,128)S(1)} %bitcast.29, f32[4,64,512]{2,1,0:T(8,128)S(1)} %bitcast.27, f32[4,32,8,512]{3,2,1,0:T(8,128)S(1)} %get-tuple-element.8.inv_ref, ...), custom_call_target="tpu_custom_call", output_to_operand_aliasing={{}: (7, {})} | custom-call | flops 44000000 | bytes 9200000 | tf_op jit(solution)/shard_map/pallas_call | solution.py:330
  207.8 21.5 %shard_map.99.rest_0_ = f32[24,128,512]{2,1,0:T(8,128)} custom-call(s32[25]{0:T(128)S(1)} %pad_add_fusion.table_ref, f32[24,128,512]{2,1,0:T(8,128)} %bitcast.40, f32[4,64,512]{2,1,0:T(8,128)S(1)} %bitcast.31, f32[4,64,512]{2,1,0:T(8,128)S(1)} %bitcast.28, f32[4,32,8,512]{3,2,1,0:T(8,128)S(1)} %get-tuple-element.8.inv_ref, ...), custom_call_target="tpu_custom_call", output_to_operand_aliasing={{}: (7, {})} | custom-call | flops 44000000 | bytes 9200000 | tf_op jit(solution)/shard_map/pallas_call | solution.py:330
  229.3 21.5 %shard_map.100 = f32[24,128,512]{2,1,0:T(8,128)} custom-call(s32[25]{0:T(128)S(1)} %pad_add_fusion.table_ref, f32[24,128,512]{2,1,0:T(8,128)} %bitcast.41, f32[4,64,512]{2,1,0:T(8,128)S(1)} %bitcast.32, f32[4,64,512]{2,1,0:T(8,128)S(1)} %bitcast.30, f32[4,32,8,512]{3,2,1,0:T(8,128)S(1)} %get-tuple-element.8.inv_ref, ...), custom_call_target="tpu_custom_call", output_to_operand_aliasing={{}: (7, {})} | custom-call | flops 44000000 | bytes 9200000 | tf_op jit(solution)/shard_map/pallas_call | solution.py:330
  (25 shorter events, 2.2 us)
Async XLA Ops:
  0.6 29.0 %copy-start.3 = (s32[8]{0:T(128)S(1)}, s32[8]{0:T(128)}, u32[]{:S(2)}) copy-start(s32[8]{0:T(128)} %param.10) | copy-start | bytes 100
  0.6 56.8 %copy-start.2 = (f32[1,16,512]{2,1,0:T(8,128)S(1)}, f32[1,16,512]{2,1,0:T(8,128)}, u32[]{:S(2)}) copy-start(f32[1,16,512]{2,1,0:T(8,128)} %param.9) | copy-start | bytes 98308
  0.7 56.8 %copy-start.1 = (f32[1,16,512]{2,1,0:T(8,128)S(1)}, f32[1,16,512]{2,1,0:T(8,128)}, u32[]{:S(2)}) copy-start(f32[1,16,512]{2,1,0:T(8,128)} %param.8) | copy-start | bytes 98308
  0.7 56.8 %copy-start = (f32[1,16,512]{2,1,0:T(8,128)S(1)}, f32[1,16,512]{2,1,0:T(8,128)}, u32[]{:S(2)}) copy-start(f32[1,16,512]{2,1,0:T(8,128)} %param.7) | copy-start | bytes 98308
  0.7 119.5 %copy-start.4 = (s32[96]{0:T(128)S(1)}, s32[96]{0:T(128)}, u32[]{:S(2)}) copy-start(s32[96]{0:T(128)} %param.11) | copy-start | bytes 1156
  5.9 15.7 %collective-permute-start.11 = (f32[4,8,8,512]{3,2,1,0:T(8,128)S(1)}, f32[4,8,8,512]{3,2,1,0:T(8,128)S(1)}, u32[]{:S(2)}, u32[]{:S(2)}) collective-permute-start(f32[4,8,8,512]{3,2,1,0:T(8,128)S(1)} %get-tuple-element.14), channel_id=1, source_target_pairs={{8,0},{16,8},{24,16},{32,24},{40,32},{48,40},{56,48},{64,56},{72,6... | collective-permute-start | bytes 1572872 | tf_op jit(solution)/shard_map/ppermute | solution.py:377
  9.1 18.6 %collective-permute-start.9 = (f32[4,8,8,512]{3,2,1,0:T(8,128)S(1)}, f32[4,8,8,512]{3,2,1,0:T(8,128)S(1)}, u32[]{:S(2)}, u32[]{:S(2)}) collective-permute-start(f32[4,8,8,512]{3,2,1,0:T(8,128)S(1)} %get-tuple-element.15), channel_id=1, source_target_pairs={{8,0},{16,8},{24,16},{32,24},{40,32},{48,40},{56,48},{64,56},{72,6... | collective-permute-start | bytes 1572872 | tf_op jit(solution)/shard_map/ppermute | solution.py:377
  11.7 19.2 %collective-permute-start.8 = (f32[4,8,8,512]{3,2,1,0:T(8,128)}, f32[4,8,8,512]{3,2,1,0:T(8,128)S(1)}, u32[]{:S(2)}, u32[]{:S(2)}) collective-permute-start(f32[4,8,8,512]{3,2,1,0:T(8,128)} %get-tuple-element.16), channel_id=1, source_target_pairs={{0,8},{8,16},{16,24},{24,32},{32,40},{40,48},{48,56},{56,64},{64,7... | collective-permute-start | bytes 1572872 | tf_op jit(solution)/shard_map/ppermute | solution.py:376
  13.6 24.4 %collective-permute-start.7 = (f32[4,8,8,512]{3,2,1,0:T(8,128)}, f32[4,8,8,512]{3,2,1,0:T(8,128)S(1)}, u32[]{:S(2)}, u32[]{:S(2)}) collective-permute-start(f32[4,8,8,512]{3,2,1,0:T(8,128)} %get-tuple-element.17), channel_id=1, source_target_pairs={{8,0},{16,8},{24,16},{32,24},{40,32},{48,40},{56,48},{64,56},{72,6... | collective-permute-start | bytes 1572872 | tf_op jit(solution)/shard_map/ppermute | solution.py:377
  19.7 24.5 %collective-permute-start.6 = (f32[4,8,8,512]{3,2,1,0:T(8,128)}, f32[4,8,8,512]{3,2,1,0:T(8,128)S(1)}, u32[]{:S(2)}, u32[]{:S(2)}) collective-permute-start(f32[4,8,8,512]{3,2,1,0:T(8,128)} %get-tuple-element.18), channel_id=1, source_target_pairs={{0,8},{8,16},{16,24},{24,32},{32,40},{40,48},{48,56},{56,64},{64,7... | collective-permute-start | bytes 1572872 | tf_op jit(solution)/shard_map/ppermute | solution.py:376
  21.6 27.7 %collective-permute-start.5 = (f32[4,8,8,512]{3,2,1,0:T(8,128)}, f32[4,8,8,512]{3,2,1,0:T(8,128)S(1)}, u32[]{:S(2)}, u32[]{:S(2)}) collective-permute-start(f32[4,8,8,512]{3,2,1,0:T(8,128)} %get-tuple-element.19), channel_id=1, source_target_pairs={{8,0},{16,8},{24,16},{32,24},{40,32},{48,40},{56,48},{64,56},{72,6... | collective-permute-start | bytes 1572872 | tf_op jit(solution)/shard_map/ppermute | solution.py:377
  27.7 27.7 %collective-permute-start.10 = (f32[4,8,8,512]{3,2,1,0:T(8,128)}, f32[4,8,8,512]{3,2,1,0:T(8,128)}, u32[]{:S(2)}, u32[]{:S(2)}) collective-permute-start(f32[4,8,8,512]{3,2,1,0:T(8,128)} %get-tuple-element.25), channel_id=1, source_target_pairs={{0,8},{8,16},{16,24},{24,32},{32,40},{40,48},{48,56},{56,64},{64,7... | collective-permute-start | bytes 1572872 | tf_op jit(solution)/shard_map/ppermute | solution.py:376
  30.9 155.4 %collective-permute-start.4 = (f32[4,8,8,512]{3,2,1,0:T(8,128)}, f32[4,8,8,512]{3,2,1,0:T(8,128)S(1)}, u32[]{:S(2)}, u32[]{:S(2)}) collective-permute-start(f32[4,8,8,512]{3,2,1,0:T(8,128)} %get-tuple-element.20), channel_id=1, source_target_pairs={{0,8},{8,16},{16,24},{24,32},{32,40},{40,48},{48,56},{56,64},{64,7... | collective-permute-start | bytes 1572872 | tf_op jit(solution)/shard_map/ppermute | solution.py:376
  38.1 169.8 %collective-permute-start.3 = (f32[4,8,8,512]{3,2,1,0:T(8,128)}, f32[4,8,8,512]{3,2,1,0:T(8,128)S(1)}, u32[]{:S(2)}, u32[]{:S(2)}) collective-permute-start(f32[4,8,8,512]{3,2,1,0:T(8,128)} %get-tuple-element.21), channel_id=1, source_target_pairs={{8,0},{16,8},{24,16},{32,24},{40,32},{48,40},{56,48},{64,56},{72,6... | collective-permute-start | bytes 1572872 | tf_op jit(solution)/shard_map/ppermute | solution.py:377
  44.2 163.6 %collective-permute-start.2 = (f32[4,8,8,512]{3,2,1,0:T(8,128)}, f32[4,8,8,512]{3,2,1,0:T(8,128)S(1)}, u32[]{:S(2)}, u32[]{:S(2)}) collective-permute-start(f32[4,8,8,512]{3,2,1,0:T(8,128)} %get-tuple-element.22), channel_id=1, source_target_pairs={{0,8},{8,16},{16,24},{24,32},{32,40},{40,48},{48,56},{56,64},{64,7... | collective-permute-start | bytes 1572872 | tf_op jit(solution)/shard_map/ppermute | solution.py:376
  49.3 180.0 %collective-permute-start.1 = (f32[4,8,8,512]{3,2,1,0:T(8,128)}, f32[4,8,8,512]{3,2,1,0:T(8,128)S(1)}, u32[]{:S(2)}, u32[]{:S(2)}) collective-permute-start(f32[4,8,8,512]{3,2,1,0:T(8,128)} %get-tuple-element.23), channel_id=1, source_target_pairs={{8,0},{16,8},{24,16},{32,24},{40,32},{48,40},{56,48},{64,56},{72,6... | collective-permute-start | bytes 1572872 | tf_op jit(solution)/shard_map/ppermute | solution.py:377
  55.4 173.9 %collective-permute-start = (f32[4,8,8,512]{3,2,1,0:T(8,128)}, f32[4,8,8,512]{3,2,1,0:T(8,128)S(1)}, u32[]{:S(2)}, u32[]{:S(2)}) collective-permute-start(f32[4,8,8,512]{3,2,1,0:T(8,128)} %get-tuple-element.24), channel_id=1, source_target_pairs={{0,8},{8,16},{16,24},{24,32},{32,40},{40,48},{48,56},{56,64},{64,7... | collective-permute-start | bytes 1572872 | tf_op jit(solution)/shard_map/ppermute | solution.py:376
where the time goes:
time: 252 us; the launch traced here: 251 us
  Pallas kernels  192 us (76%)
  starting transfers between devices  41.6 us (17%)
  waiting for transfers between devices  8.43 us (3%)
  local copies, waits for them, and re-layouts  5.88 us (2%)
    pallas_call x6, Pallas kernels, tracer_chunk(): pl.pallas_call(functools.partial(tracer_kernel, base), grid_spec=pltpu.Pr...  129 us
    pallas_call x1, Pallas kernels, gather_fields(): pl.pallas_call(gather_kernel, out_shape=jax.ShapeDtypeStruct((n_comp, 3,...  45.5 us
    ppermute x6, starting transfers between devices, on_device(): highs.append(lax.ppermute(part[:, :, :HALO], 'band', backward))  30 us
    pallas_call x1, Pallas kernels, dynamics(): pl.pallas_call(dynamics_kernel, out_shape=(rows, rows, rows, jax.ShapeDty...  17.3 us
    ppermute x6, starting transfers between devices, on_device(): lows.append(lax.ppermute(part[:, :, ROWS - HALO:], 'band', forward))  11.5 us
    ppermute x6, waiting for transfers between devices, on_device(): highs.append(lax.ppermute(part[:, :, :HALO], 'band', backward))  8.42 us
    slice x1, local copies, waits for them, and re-layouts, on_device(): highs.append(lax.ppermute(part[:, :, :HALO], 'band', backward))  5.22 us
  transfers between devices with their start and end apart: 12, of which 2 were waited for; matrix products, arithmetic and copies ran while one was open for 1% of the time, Pallas kernels for 68%

commit v1 on v0

--- a/solution.py
+++ b/solution.py
@@ -8,7 +8,7 @@
 from jax.sharding import PartitionSpec as P
 
 STEPS = 4
-CHUNK = 4
+CHUNK = 8
 HALO = 8
 ROWS = 16
 EXT = ROWS + 2 * HALO
@@ -40,10 +40,37 @@
 
 
 def roll(value, shift):
-    return pltpu.roll(value, shift % value.shape[-1], value.ndim - 1)
-
-
-def gather_kernel(h_ref, u_ref, v_ref, out_ref, send_sem, recv_sem, halo_send, halo_recv):
+    count = NX // 128
+    tiles = [value[..., columns(i)] for i in range(count)]
+    made = []
+    for i in range(count):
+        turns, at = divmod(i - shift, count)
+        tile = tiles[at]
+        if turns:
+            tile = pltpu.roll(tile, (-turns) % 128, tile.ndim - 1)
+        made.append(tile)
+    return jnp.concatenate(made, axis=-1)
+
+
+def dealing():
+    source = lax.broadcasted_iota(jnp.int32, (NX, NX), 0)
+    place = lax.broadcasted_iota(jnp.int32, (NX, NX), 1)
+    deal = source == (place % 128) * (NX // 128) + place // 128
+    return deal.astype(jnp.bfloat16)
+
+
+def permuted(value, table):
+    total = None
+    rest = value
+    for part in range(3):
+        piece = rest.astype(jnp.bfloat16)
+        moved = jnp.dot(piece, table, preferred_element_type=jnp.float32)
+        total = moved if total is None else total + moved
+        rest = rest - piece.astype(jnp.float32)
+    return total
+
+
+def gather_kernel(h_ref, u_ref, v_ref, deal_ref, out_ref, send_sem, recv_sem, halo_send, halo_recv):
     n_comp, n_band = lax.axis_size("comp"), lax.axis_size("band")
     level, band = lax.axis_index("comp"), lax.axis_index("band")
     has_low, has_high = band > 0, band < n_band - 1
@@ -62,7 +89,7 @@
         pl.semaphore_signal(barrier, inc=1, device_id={"band": band + 1}, device_id_type=MESH_ID)
 
     for f, ref in enumerate((h_ref, u_ref, v_ref)):
-        out_ref[level, f, HALO : HALO + ROWS, :] = ref[...]
+        out_ref[level, f, HALO : HALO + ROWS, :] = permuted(ref[...], deal_ref[...])
 
     @pl.when(jnp.logical_not(has_low))
     def _():
@@ -145,12 +172,12 @@
             copy(piece, p, lax.rem(level + n_comp - p, n_comp)).wait_recv()
 
 
-def gather_fields(height, zonal, merid):
+def gather_fields(height, zonal, merid, deal):
     n_comp = lax.axis_size("comp")
     return pl.pallas_call(
         gather_kernel,
         out_shape=jax.ShapeDtypeStruct((n_comp, 3, EXT, NX), jnp.float32),
-        in_specs=[pl.BlockSpec(memory_space=pltpu.VMEM)] * 3,
+        in_specs=[pl.BlockSpec(memory_space=pltpu.VMEM)] * 4,
         out_specs=pl.BlockSpec(memory_space=pltpu.VMEM),
         scratch_shapes=[
             pltpu.SemaphoreType.DMA((3, n_comp)),
@@ -161,10 +188,10 @@
         compiler_params=pltpu.CompilerParams(
             collective_id=0, has_side_effects=True, vmem_limit_bytes=16 * 1024 * 1024
         ),
-    )(height, zonal, merid)
-
-
-def dynamics_kernel(where_ref, g_ref, inv_ref, east_ref, south_ref, last_ref, h_buf, u_buf, v_buf, stage):
+    )(height, zonal, merid, deal)
+
+
+def dynamics_kernel(where_ref, g_ref, back_ref, inv_ref, east_ref, south_ref, last_ref, h_buf, u_buf, v_buf, stage, picked_ref):
     first_row, level, total_rows = where_ref[0], where_ref[1], where_ref[2]
     stride = 3 * EXT
 
@@ -215,47 +242,53 @@
             v_buf[j] = v - time_step * (coriolis * u + 0.5 * (geo_after - geo_before))
             return h_after, v_after, geo, geo_after, south_after
 
-        lax.fori_loop(
-            low, high, row, (h_here, v_here, geopot(h_before), geopot(h_here), south)
-        )
+        carry = (h_here, v_here, geopot(h_before), geopot(h_here), south)
+        for j in range(low, high):
+            carry = row(j, carry)
 
     own = lax.broadcasted_iota(jnp.int32, (LEVELS, NX), 0) == level
     for f, buf in enumerate((h_buf, u_buf, v_buf)):
         for j in range(ROWS):
             picked = jnp.where(own, buf[HALO + j], 0.0)
-            last_ref[f, pl.ds(j, 1), :] = jnp.sum(picked, axis=0, keepdims=True)
-
-
-def dynamics(where, gathered):
+            picked_ref[pl.ds(f * ROWS + j, 1), :] = jnp.sum(picked, axis=0, keepdims=True)
+    last_ref[...] = permuted(picked_ref[...], back_ref[...])
+
+
+def dynamics(where, gathered, back):
     rows = jax.ShapeDtypeStruct((STEPS, EXT, LEVELS, NX), jnp.float32)
     vmem = pl.BlockSpec(memory_space=pltpu.VMEM)
     return pl.pallas_call(
         dynamics_kernel,
-        out_shape=(rows, rows, rows, jax.ShapeDtypeStruct((3, ROWS, NX), jnp.float32)),
-        in_specs=[pl.BlockSpec(memory_space=pltpu.SMEM), vmem],
+        out_shape=(rows, rows, rows, jax.ShapeDtypeStruct((3 * ROWS, NX), jnp.float32)),
+        in_specs=[pl.BlockSpec(memory_space=pltpu.SMEM), vmem, vmem],
         out_specs=(vmem,) * 4,
         scratch_shapes=[pltpu.VMEM((EXT, LEVELS, NX), jnp.float32)] * 3
-        + [pltpu.VMEM((NX // 128, LEVELS * 3 * EXT, 128), jnp.float32)],
+        + [
+            pltpu.VMEM((NX // 128, LEVELS * 3 * EXT, 128), jnp.float32),
+            pltpu.VMEM((3 * ROWS, NX), jnp.float32),
+        ],
         compiler_params=pltpu.CompilerParams(vmem_limit_bytes=VMEM_LIMIT),
         cost_estimate=pl.CostEstimate(
             flops=10_000_000, bytes_accessed=8_000_000, transcendentals=0
         ),
-    )(where, gathered)
-
-
-def tracer_kernel(base, table_ref, m_ref, low_ref, high_ref, inv_ref, east_ref, south_ref, *rest):
+    )(where, gathered, back)
+
+
+def tracer_kernel(
+    base, table_ref, m_ref, low_ref, high_ref, deal_ref, back_ref, inv_ref, east_ref, south_ref, *rest
+):
     out_ref, buf, stage, low_stage, high_stage = rest[-5:]
     slot = base + pl.program_id(0)
     live = slot < table_ref[0]
     limited = table_ref[1 + slot] > 0
-
-    def face(a_out, a, b, b_out, bounded):
+    tiles = NX // 128
+
+    def face(a_out, a, b, b_out):
         raw = (7.0 / 12.0) * (a + b) - (1.0 / 12.0) * (a_out + b_out)
-        if not bounded:
-            return raw
-        return jnp.maximum(jnp.minimum(raw, jnp.maximum(a, b)), jnp.minimum(a, b))
-
-    def advance(bounded):
+        bounded = jnp.maximum(jnp.minimum(raw, jnp.maximum(a, b)), jnp.minimum(a, b))
+        return jnp.where(limited, bounded, raw)
+
+    def advance():
         for step in range(STEPS):
             reach = reach_of(step)
             low, high = HALO - reach, HALO + ROWS + reach
@@ -263,65 +296,48 @@
             def ratio(j, step=step):
                 return buf[j] * inv_ref[step, j]
 
-            def row(j, carry, step=step):
-                before, here, after, south = carry
+            before, here, after = ratio(low - 1), ratio(low), ratio(low + 1)
+            south = south_ref[step, low] * face(ratio(low - 2), before, here, after)
+            for j in range(low, high):
                 beyond = ratio(j + 2)
-                south_after = south_ref[step, j + 1] * face(before, here, after, beyond, bounded)
-                east = east_ref[step, j] * face(
-                    roll(here, 1), here, roll(here, -1), roll(here, -2), bounded
-                )
+                south_after = south_ref[step, j + 1] * face(before, here, after, beyond)
+                east = east_ref[step, j] * face(roll(here, 1), here, roll(here, -1), roll(here, -2))
                 new = buf[j] - ((east - roll(east, 1)) + (south_after - south))
                 if step < STEPS - 1:
                     buf[j] = new
                 else:
-                    for i in range(NX // 128):
+                    for i in range(tiles):
                         stage[i, pl.ds(j - HALO, LEVELS, stride=ROWS), :] = new[:, columns(i)]
-                return here, after, beyond, south_after
-
-            def rows(i, carry):
-                for k in range(4):
-                    carry = row(low + i * 4 + k, carry)
-                return carry
-
-            start = [ratio(low + k) for k in (-2, -1, 0, 1)]
-            south = south_ref[step, low] * face(*start, bounded)
-            lax.fori_loop(0, (high - low) // 4, rows, (*start[1:], south))
+                before, here, after, south = here, after, beyond, south_after
 
     @pl.when(live)
     def _():
-        for i in range(NX // 128):
-            stage[i] = m_ref[0, :, columns(i)]
-            low_stage[i] = low_ref[0, :, columns(i)]
-            high_stage[i] = high_ref[0, :, columns(i)]
+        for ref, to in ((m_ref, stage), (low_ref, low_stage), (high_ref, high_stage)):
+            dealt = permuted(ref[0], deal_ref[...])
+            for i in range(tiles):
+                to[i] = dealt[:, columns(i)]
         for j in range(HALO):
             buf[j] = level_rows(low_stage, j, HALO)
             buf[HALO + ROWS + j] = level_rows(high_stage, j, HALO)
         for j in range(ROWS):
             buf[HALO + j] = level_rows(stage, j, ROWS)
-
-        @pl.when(limited)
-        def _():
-            advance(True)
-
-        @pl.when(jnp.logical_not(limited))
-        def _():
-            advance(False)
-
-        for i in range(NX // 128):
-            out_ref[0, :, columns(i)] = stage[i]
+        advance()
+        final = jnp.concatenate([stage[i] for i in range(tiles)], axis=1)
+        out_ref[0] = permuted(final, back_ref[...])
 
     @pl.when(jnp.logical_not(live))
     def _():
         out_ref[...] = jnp.zeros_like(out_ref)
 
 
-def tracer_chunk(base, count, table, mass, low, high, fluxes, so_far):
+def tracer_chunk(base, count, table, mass, low, high, tables, fluxes, so_far):
     slots = mass.shape[0]
     whole = pl.BlockSpec((STEPS, EXT, LEVELS, NX), lambda i, t: (0, 0, 0, 0), pipeline_mode=pl.Buffered(1))
     block = pl.BlockSpec((1, LEVELS * ROWS, NX), lambda i, t: (base + i, 0, 0))
     side = pl.BlockSpec((1, LEVELS * HALO, NX), lambda i, t: (i, 0, 0))
-    operands = [table, mass, low, high, *fluxes]
-    specs = [block, side, side, whole, whole, whole]
+    square = pl.BlockSpec((NX, NX), lambda i, t: (0, 0), pipeline_mode=pl.Buffered(1))
+    operands = [table, mass, low, high, *tables, *fluxes]
+    specs = [block, side, side, square, square, whole, whole, whole]
     aliases = {}
     if so_far is not None:
         aliases = {len(operands): 0}
@@ -367,24 +383,28 @@
     forward = [(i, i + 1) for i in range(n_band - 1)]
     backward = [(i + 1, i) for i in range(n_band - 1)]
 
+    deal = dealing()
+    back = deal.T
     gathered = gather_fields(
-        layer_mass.reshape(ROWS, NX), zonal_wind.reshape(ROWS, NX), merid_wind.reshape(ROWS, NX)
-    )
+        layer_mass.reshape(ROWS, NX), zonal_wind.reshape(ROWS, NX), merid_wind.reshape(ROWS, NX), deal
+    )
+    mass, gathered = lax.optimization_barrier((tracer_mass, gathered))
     lows, highs = [], []
     for base in range(0, slots, CHUNK):
-        part = tracer_mass[base : base + CHUNK]
+        part = mass[base : base + CHUNK]
         lows.append(lax.ppermute(part[:, :, ROWS - HALO :], "band", forward))
         highs.append(lax.ppermute(part[:, :, :HALO], "band", backward))
 
-    *fluxes, last = dynamics(where, gathered.reshape(n_comp * 3 * EXT, NX))
+    *fluxes, last = dynamics(where, gathered.reshape(n_comp * 3 * EXT, NX), back)
     mass = tracer_mass.reshape(slots, LEVELS * ROWS, NX)
     out = None
     for k, base in enumerate(range(0, slots, CHUNK)):
         low = lows[k].reshape(CHUNK, LEVELS * HALO, NX)
         high = highs[k].reshape(CHUNK, LEVELS * HALO, NX)
-        out = tracer_chunk(base, CHUNK, table, mass, low, high, fluxes, out)
+        out = tracer_chunk(base, CHUNK, table, mass, low, high, (deal, back), fluxes, out)
     tracers = out.reshape(tracer_mass.shape)
-    return tracers, last[0][None], last[1][None], last[2][None]
+    last = last.reshape(3, 1, ROWS, NX)
+    return tracers, last[0], last[1], last[2]
 
 
 def solution(mesh):

time: 252 us -> 145 us (0.58)
  the two profiles are of different devices: /device:TPU:42 before, /device:TPU:91 now
where the time goes in v1:
time: 145 us; the launch traced here: 144 us
  Pallas kernels  101 us (70%)
  starting transfers between devices  19.9 us (14%)
  local copies, waits for them, and re-layouts  10.4 us (7%)
  waiting for transfers between devices  9.14 us (6%)
  other arithmetic  2.99 us (2%)
    pallas_call x3, Pallas kernels, tracer_chunk(): pl.pallas_call(functools.partial(tracer_kernel, base), grid_spec=pltpu.Pr...  71.5 us
    pallas_call x1, Pallas kernels, gather_fields(): pl.pallas_call(gather_kernel, out_shape=jax.ShapeDtypeStruct((n_comp, 3,...  23.3 us
    ppermute x3, starting transfers between devices, on_device(): lows.append(lax.ppermute(part[:, :, ROWS - HALO:], 'band', forward))  13.8 us
    ppermute x3, waiting for transfers between devices, on_device(): highs.append(lax.ppermute(part[:, :, :HALO], 'band', backward))  9.13 us
    pallas_call x1, Pallas kernels, dynamics(): pl.pallas_call(dynamics_kernel, out_shape=(rows, rows, rows, jax.ShapeDty...  6.54 us
    ppermute x3, starting transfers between devices, on_device(): highs.append(lax.ppermute(part[:, :, :HALO], 'band', backward))  6.13 us
    slice x1, local copies, waits for them, and re-layouts, on_device(): highs.append(lax.ppermute(part[:, :, :HALO], 'band', backward))  5.25 us
    unnamed x14, local copies, waits for them, and re-layouts  4.48 us
  transfers between devices with their start and end apart: 6, of which 1 were waited for; matrix products, arithmetic and copies ran while one was open for 2% of the time, Pallas kernels for 37%

profile of v1, /device:TPU:91, one launch (start us, length us, event | category | flops | bytes accessed | tf_op | source)
XLA Modules:
  0.0 144.5 jit_solution(1061930597720451643)
XLA Ops:
  0.7 0.7 fusion.1
  1.4 0.7 copy-done.2
  2.1 0.8 copy-done.3
  2.9 0.8 copy-done.4
  3.7 23.3 %shard_map.93 = f32[8,3,32,512]{3,2,1,0:T(8,128)S(1)} custom-call(f32[16,512]{1,0:T(8,128)S(1)} %bitcast.23, f32[16,512]{1,0:T(8,128)S(1)} %bitcast.24, f32[16,512]{1,0:T(8,128)S(1)} %bitcast.25, bf16[512,512]{1,0:T(8,128)(2,1)S(1)} %get-tuple-element.28.deal_ref), custom_call_target="tpu_custom_call" | custom-call | tf_op jit(solution)/shard_map/pallas_call | solution.py:177
  27.0 5.2 %fusion.10 = (f32[8,8,8,512]{3,2,1,0:T(8,128)S(1)}, f32[8,8,8,512]{3,2,1,0:T(8,128)}, f32[8,8,8,512]{3,2,1,0:T(8,128)}, f32[8,8,8,512]{3,2,1,0:T(8,128)}, f32[8,8,8,512]{3,2,1,0:T(8,128)}, /*index=5*/f32[8,8,8,512]{3,2,1,0:T(8,128)}) fusion(f32[24,8,16,512]{3,2,1,0:T(8,128)} %param.6), kind=kLoop, calls=%fused_computation.26 | loop fusion | bytes 12582912 | tf_op jit(solution)/shard_map/slice | solution.py:396
  32.2 2.3 %collective-permute-start.5 = (f32[8,8,8,512]{3,2,1,0:T(8,128)S(1)}, f32[8,8,8,512]{3,2,1,0:T(8,128)S(1)}, u32[]{:S(2)}, u32[]{:S(2)}) collective-permute-start(f32[8,8,8,512]{3,2,1,0:T(8,128)S(1)} %get-tuple-element.18), channel_id=1, source_target_pairs={{8,0},{16,8},{24,16},{32,24},{40,32},{48,40},{56,48},{64,56},{72,6... | collective-permute-start | bytes 3145736 | tf_op jit(solution)/shard_map/ppermute | solution.py:396
  34.5 5.7 %collective-permute-start.4 = (f32[8,8,8,512]{3,2,1,0:T(8,128)}, f32[8,8,8,512]{3,2,1,0:T(8,128)}, u32[]{:S(2)}, u32[]{:S(2)}) collective-permute-start(f32[8,8,8,512]{3,2,1,0:T(8,128)} %get-tuple-element.19), channel_id=1, source_target_pairs={{0,8},{8,16},{16,24},{24,32},{32,40},{40,48},{48,56},{56,64},{64,7... | collective-permute-start | bytes 3145736 | tf_op jit(solution)/shard_map/ppermute | solution.py:395
  40.2 1.9 %collective-permute-start.3 = (f32[8,8,8,512]{3,2,1,0:T(8,128)}, f32[8,8,8,512]{3,2,1,0:T(8,128)}, u32[]{:S(2)}, u32[]{:S(2)}) collective-permute-start(f32[8,8,8,512]{3,2,1,0:T(8,128)} %get-tuple-element.20), channel_id=1, source_target_pairs={{8,0},{16,8},{24,16},{32,24},{40,32},{48,40},{56,48},{64,56},{72,6... | collective-permute-start | bytes 3145736 | tf_op jit(solution)/shard_map/ppermute | solution.py:396
  42.1 6.0 %collective-permute-start.2 = (f32[8,8,8,512]{3,2,1,0:T(8,128)}, f32[8,8,8,512]{3,2,1,0:T(8,128)}, u32[]{:S(2)}, u32[]{:S(2)}) collective-permute-start(f32[8,8,8,512]{3,2,1,0:T(8,128)} %get-tuple-element.21), channel_id=1, source_target_pairs={{0,8},{8,16},{16,24},{24,32},{32,40},{40,48},{48,56},{56,64},{64,7... | collective-permute-start | bytes 3145736 | tf_op jit(solution)/shard_map/ppermute | solution.py:395
  48.2 1.9 %collective-permute-start.1 = (f32[8,8,8,512]{3,2,1,0:T(8,128)}, f32[8,8,8,512]{3,2,1,0:T(8,128)}, u32[]{:S(2)}, u32[]{:S(2)}) collective-permute-start(f32[8,8,8,512]{3,2,1,0:T(8,128)} %get-tuple-element.22), channel_id=1, source_target_pairs={{8,0},{16,8},{24,16},{32,24},{40,32},{48,40},{56,48},{64,56},{72,6... | collective-permute-start | bytes 3145736 | tf_op jit(solution)/shard_map/ppermute | solution.py:396
  50.1 9.1 %collective-permute-done.5 = f32[8,8,8,512]{3,2,1,0:T(8,128)S(1)} collective-permute-done((f32[8,8,8,512]{3,2,1,0:T(8,128)S(1)}, f32[8,8,8,512]{3,2,1,0:T(8,128)S(1)}, u32[]{:S(2)}, u32[]{:S(2)}) %collective-permute-start.5) | collective-permute-done | bytes 1048608 | tf_op jit(solution)/shard_map/ppermute | solution.py:396
  59.2 1.0 copy-done
  60.2 2.1 %collective-permute-start = (f32[8,8,8,512]{3,2,1,0:T(8,128)}, f32[8,8,8,512]{3,2,1,0:T(8,128)}, u32[]{:S(2)}, u32[]{:S(2)}) collective-permute-start(f32[8,8,8,512]{3,2,1,0:T(8,128)} %get-tuple-element.23), channel_id=1, source_target_pairs={{0,8},{8,16},{16,24},{24,32},{32,40},{40,48},{48,56},{56,64},{64,7... | collective-permute-start | bytes 3145736 | tf_op jit(solution)/shard_map/ppermute | solution.py:395
  62.4 6.5 %shard_map.94 = (f32[4,32,8,512]{3,2,1,0:T(8,128)S(1)}, f32[4,32,8,512]{3,2,1,0:T(8,128)}, f32[4,32,8,512]{3,2,1,0:T(8,128)}, f32[48,512]{1,0:T(8,128)S(1)}) custom-call(s32[3]{0:T(128)S(1)} %pad_add_fusion.1.where_ref, f32[768,512]{1,0:T(8,128)S(1)} %bitcast.21, bf16[512,512]{1,0:T(8,128)(2,1)S(1)} %get-tuple-element.27.back_ref), custom_call_target="tpu_custom_call" | custom-call | flops 10000000 | bytes 8000000 | tf_op jit(solution)/shard_map/pallas_call | solution.py:260
  68.9 0.6 fusion.8
  69.6 0.6 iota_add_fusion
  70.2 0.2 select_reduce_fusion
  70.4 0.7 pad_add_fusion.table_ref
  71.1 0.6 slice_bitcast_fusion
  71.8 1.2 copy-done.1
  73.0 23.8 %shard_map.95.rest_0_ = f32[24,128,512]{2,1,0:T(8,128)} custom-call(s32[25]{0:T(128)S(1)} %pad_add_fusion.table_ref, f32[24,128,512]{2,1,0:T(8,128)} %bitcast.26, f32[8,64,512]{2,1,0:T(8,128)} %bitcast.12.low_ref, f32[8,64,512]{2,1,0:T(8,128)S(1)} %bitcast.22, bf16[512,512]{1,0:T(8,128)(2,1)S(1)} %get-tuple-element.28.deal_ref, ...), custom_call_target="tpu_custom_call" | custom-call | flops 88000000 | bytes 12400000 | tf_op jit(solution)/shard_map/pallas_call | solution.py:346
  96.8 23.9 %shard_map.96.rest_0_ = f32[24,128,512]{2,1,0:T(8,128)} custom-call(s32[25]{0:T(128)S(1)} %pad_add_fusion.table_ref, f32[24,128,512]{2,1,0:T(8,128)} %bitcast.27, f32[8,64,512]{2,1,0:T(8,128)} %bitcast.10.low_ref, f32[8,64,512]{2,1,0:T(8,128)} %bitcast.11.high_ref, bf16[512,512]{1,0:T(8,128)(2,1)S(1)} %get-tuple-element.28.deal_ref, ...), custom_call_target="tpu_custom_call", output_to_operand_aliasing={{}: (9, {})} | custom-call | flops 88000000 | bytes 12400000 | tf_op jit(solution)/shard_map/pallas_call | solution.py:346
  120.6 23.9 %shard_map.97 = f32[24,128,512]{2,1,0:T(8,128)} custom-call(s32[25]{0:T(128)S(1)} %pad_add_fusion.table_ref, f32[24,128,512]{2,1,0:T(8,128)} %bitcast.28, f32[8,64,512]{2,1,0:T(8,128)} %bitcast.5.low_ref, f32[8,64,512]{2,1,0:T(8,128)} %bitcast.6.high_ref, bf16[512,512]{1,0:T(8,128)(2,1)S(1)} %get-tuple-element.28.deal_ref, ...), custom_call_target="tpu_custom_call", output_to_operand_aliasing={{}: (9, {})} | custom-call | flops 88000000 | bytes 12400000 | tf_op jit(solution)/shard_map/pallas_call | solution.py:346
  (18 shorter events, 0.1 us)
Async XLA Ops:
  1.4 0.8 copy-start.2
  2.1 0.8 copy-start.3
  2.9 0.8 copy-start.4
  27.0 42.0 %copy-start.5 = (s32[8]{0:T(128)S(1)}, s32[8]{0:T(128)}, u32[]{:S(2)}) copy-start(s32[8]{0:T(128)} %param.10) | copy-start | bytes 100
  27.0 43.3 %copy-start.6 = (s32[96]{0:T(128)S(1)}, s32[96]{0:T(128)}, u32[]{:S(2)}) copy-start(s32[96]{0:T(128)} %param.11) | copy-start | bytes 1156
  32.2 27.0 %collective-permute-start.5 = (f32[8,8,8,512]{3,2,1,0:T(8,128)S(1)}, f32[8,8,8,512]{3,2,1,0:T(8,128)S(1)}, u32[]{:S(2)}, u32[]{:S(2)}) collective-permute-start(f32[8,8,8,512]{3,2,1,0:T(8,128)S(1)} %get-tuple-element.18), channel_id=1, source_target_pairs={{8,0},{16,8},{24,16},{32,24},{40,32},{48,40},{56,48},{64,56},{72,6... | collective-permute-start | bytes 3145736 | tf_op jit(solution)/shard_map/ppermute | solution.py:396
  34.5 37.3 %collective-permute-start.4 = (f32[8,8,8,512]{3,2,1,0:T(8,128)}, f32[8,8,8,512]{3,2,1,0:T(8,128)}, u32[]{:S(2)}, u32[]{:S(2)}) collective-permute-start(f32[8,8,8,512]{3,2,1,0:T(8,128)} %get-tuple-element.19), channel_id=1, source_target_pairs={{0,8},{8,16},{16,24},{24,32},{32,40},{40,48},{48,56},{56,64},{64,7... | collective-permute-start | bytes 3145736 | tf_op jit(solution)/shard_map/ppermute | solution.py:395
  40.2 56.6 %collective-permute-start.3 = (f32[8,8,8,512]{3,2,1,0:T(8,128)}, f32[8,8,8,512]{3,2,1,0:T(8,128)}, u32[]{:S(2)}, u32[]{:S(2)}) collective-permute-start(f32[8,8,8,512]{3,2,1,0:T(8,128)} %get-tuple-element.20), channel_id=1, source_target_pairs={{8,0},{16,8},{24,16},{32,24},{40,32},{48,40},{56,48},{64,56},{72,6... | collective-permute-start | bytes 3145736 | tf_op jit(solution)/shard_map/ppermute | solution.py:396
  42.1 54.6 %collective-permute-start.2 = (f32[8,8,8,512]{3,2,1,0:T(8,128)}, f32[8,8,8,512]{3,2,1,0:T(8,128)}, u32[]{:S(2)}, u32[]{:S(2)}) collective-permute-start(f32[8,8,8,512]{3,2,1,0:T(8,128)} %get-tuple-element.21), channel_id=1, source_target_pairs={{0,8},{8,16},{16,24},{24,32},{32,40},{40,48},{48,56},{56,64},{64,7... | collective-permute-start | bytes 3145736 | tf_op jit(solution)/shard_map/ppermute | solution.py:395
  48.2 72.5 %collective-permute-start.1 = (f32[8,8,8,512]{3,2,1,0:T(8,128)}, f32[8,8,8,512]{3,2,1,0:T(8,128)}, u32[]{:S(2)}, u32[]{:S(2)}) collective-permute-start(f32[8,8,8,512]{3,2,1,0:T(8,128)} %get-tuple-element.22), channel_id=1, source_target_pairs={{8,0},{16,8},{24,16},{32,24},{40,32},{48,40},{56,48},{64,56},{72,6... | collective-permute-start | bytes 3145736 | tf_op jit(solution)/shard_map/ppermute | solution.py:396
  59.2 1.0 copy-start
  60.2 60.4 %collective-permute-start = (f32[8,8,8,512]{3,2,1,0:T(8,128)}, f32[8,8,8,512]{3,2,1,0:T(8,128)}, u32[]{:S(2)}, u32[]{:S(2)}) collective-permute-start(f32[8,8,8,512]{3,2,1,0:T(8,128)} %get-tuple-element.23), channel_id=1, source_target_pairs={{0,8},{8,16},{16,24},{24,32},{32,40},{40,48},{48,56},{56,64},{64,7... | collective-permute-start | bytes 3145736 | tf_op jit(solution)/shard_map/ppermute | solution.py:395
  71.8 1.2 copy-start.1

commit v2 on v1

v2 whole, which is shorter than its diff:
```python
import jax
import jax.numpy as jnp
from jax import lax
from jax.experimental import pallas as pl
from jax.experimental.pallas import tpu as pltpu
from jax.sharding import PartitionSpec as P

STEPS = 4
HALO = 8
ROWS = 16
EXT = ROWS + 2 * HALO
LEVELS = 8
NX = 512
SLOTS = 24
BLOCK = 4
EARLY = 4
TILES = NX // 128
MESH_ID = pl.DeviceIdType.MESH
VMEM_LIMIT = 48 * 1024 * 1024

time_step = 0.1
gravity = 0.25
coriolis = 0.5
mass_floor = 0.5


def reach_of(step):
    return 2 * (STEPS - 1 - step)


def columns(i):
    return slice(128 * i, 128 * i + 128)


def level_rows(stage, first, stride):
    tiles = [
        stage[i, pl.ds(first, LEVELS, stride=stride), :] for i in range(NX // 128)
    ]
    return jnp.concatenate(tiles, axis=1)


def roll(value, shift):
    count = NX // 128
    tiles = [value[..., columns(i)] for i in range(count)]
    made = []
    for i in range(count):
        turns, at = divmod(i - shift, count)
        tile = tiles[at]
        if turns and tile.ndim == 3:
            turned = [pltpu.roll(tile[k], (-turns) % 128, 1) for k in range(tile.shape[0])]
            tile = jnp.stack(turned)
        elif turns:
            tile = pltpu.roll(tile, (-turns) % 128, 1)
        made.append(tile)
    return jnp.concatenate(made, axis=-1)


def dealing():
    source = lax.broadcasted_iota(jnp.int32, (NX, NX), 0)
    place = lax.broadcasted_iota(jnp.int32, (NX, NX), 1)
    deal = source == (place % 128) * (NX // 128) + place // 128
    return deal.astype(jnp.bfloat16)


def permuted(value, table):
    total = None
    rest = value
    for part in range(3):
        piece = rest.astype(jnp.bfloat16)
        moved = jnp.dot(piece, table, preferred_element_type=jnp.float32)
        total = moved if total is None else total + moved
        rest = rest - piece.astype(jnp.float32)
    return total


def dynamics(fields, back_ref, inv_ref, east_ref, south_ref, last_refs, h_buf, u_buf, v_buf, stage, picked_ref):
    level, band = lax.axis_index("comp"), lax.axis_index("band")
    first_row, total_rows = band * ROWS, lax.axis_size("band") * ROWS
    stride = 3 * EXT

    for k in range(LEVELS):
        for f in range(3):
            rows = slice((k * 3 + f) * EXT, (k * 3 + f + 1) * EXT)
            for i in range(TILES):
                stage[i, rows, :] = fields[k, f, :, columns(i)]

    @pl.loop(0, EXT)
    def _(j):
        for f, buf in enumerate((h_buf, u_buf, v_buf)):
            buf[j] = level_rows(stage, f * EXT + j, stride)

    depth = lax.broadcasted_iota(jnp.int32, (LEVELS, NX), 0)

    def geopot(h):
        total = h
        for gap in (1, 2, 4):
            moved = pltpu.roll(total, LEVELS - gap, 0)
            total = total + jnp.where(depth < LEVELS - gap, moved, 0.0)
        return gravity * total

    def south_flux(h_a, h_b, v_a, v_b, face):
        at = first_row + face - HALO
        inside = jnp.logical_and(at > 0, at < total_rows)
        scale = jnp.where(inside, 0.25 * time_step, 0.0)
        return scale * ((v_a + v_b) * (h_a + h_b))

    for step in range(STEPS):
        reach = reach_of(step)
        low, high = HALO - reach, HALO + ROWS + reach
        for j in (low - 2, low - 1, high, high + 1):
            inv_ref[step, j] = 1.0 / jnp.maximum(h_buf[j], mass_floor)
        h_before, h_here = h_buf[low - 1], h_buf[low]
        v_before, v_here = v_buf[low - 1], v_buf[low]
        south = south_flux(h_before, h_here, v_before, v_here, low)
        south_ref[step, low] = south

        def row(j, carry, step=step):
            h, v, geo_before, geo, south = carry
            h_after, v_after, u = h_buf[j + 1], v_buf[j + 1], u_buf[j]
            geo_after = geopot(h_after)
            south_after = south_flux(h, h_after, v, v_after, j + 1)
            east = (0.25 * time_step) * ((u + roll(u, -1)) * (h + roll(h, -1)))
            inv_ref[step, j] = 1.0 / jnp.maximum(h, mass_floor)
            east_ref[step, j] = east
            south_ref[step, j + 1] = south_after
            h_buf[j] = h - ((east - roll(east, 1)) + (south_after - south))
            u_buf[j] = u + time_step * (coriolis * v - 0.5 * (roll(geo, -1) - roll(geo, 1)))
            v_buf[j] = v - time_step * (coriolis * u + 0.5 * (geo_after - geo_before))
            return h_after, v_after, geo, geo_after, south_after

        carry = (h_here, v_here, geopot(h_before), geopot(h_here), south)
        for j in range(low, high):
            carry = row(j, carry)

    own = lax.broadcasted_iota(jnp.int32, (LEVELS, NX), 0) == level
    for f, buf in enumerate((h_buf, u_buf, v_buf)):
        for j in range(ROWS):
            picked = jnp.where(own, buf[HALO + j], 0.0)
            picked_ref[pl.ds(f * ROWS + j, 1), :] = jnp.sum(picked, axis=0, keepdims=True)
    last = permuted(picked_ref[...], back_ref[...])
    for f in range(3):
        last_refs[f][...] = last[f * ROWS : (f + 1) * ROWS]


def advance_slot(limited, buf, stage, inv_ref, east_ref, south_ref):
    def face(a_out, a, b, b_out):
        raw = (7.0 / 12.0) * (a + b) - (1.0 / 12.0) * (a_out + b_out)
        bounded = jnp.maximum(jnp.minimum(raw, jnp.maximum(a, b)), jnp.minimum(a, b))
        return jnp.where(limited, bounded, raw)

    for step in range(STEPS):
        reach = reach_of(step)
        low, high = HALO - reach, HALO + ROWS + reach

        def ratios(j, n, step=step):
            return buf[j : j + n] * inv_ref[step, j : j + n]

        r = ratios(low - 2, 4)
        south = south_ref[step, low : low + 1] * face(r[0:1], r[1:2], r[2:3], r[3:4])
        r = r[1:]
        for j in range(low, high, BLOCK):
            r = jnp.concatenate([r, ratios(j + 2, BLOCK)], axis=0)
            here = r[1 : BLOCK + 1]
            after = south_ref[step, j + 1 : j + 1 + BLOCK] * face(
                r[0:BLOCK], here, r[2 : BLOCK + 2], r[3 : BLOCK + 3]
            )
            south = jnp.concatenate([south, after], axis=0)
            east = east_ref[step, j : j + BLOCK] * face(
                roll(here, 1), here, roll(here, -1), roll(here, -2)
            )
            new = buf[j : j + BLOCK] - ((east - roll(east, 1)) + (after - south[:BLOCK]))
            if step < STEPS - 1:
                buf[j : j + BLOCK] = new
            else:
                for k in range(BLOCK):
                    for i in range(TILES):
                        place = pl.ds(j + k - HALO, LEVELS, stride=ROWS)
                        stage[i, place, :] = new[k][:, columns(i)]
            r, south = r[BLOCK:], south[BLOCK:]


def kernel(
    table_ref, h_ref, u_ref, v_ref, deal_ref, back_ref, mass_ref,
    out_ref, h_out, u_out, v_out,
    fields, masses, lows, highs, inv_ref, east_ref, south_ref,
    h_buf, u_buf, v_buf, g_stage, picked_ref, buf, stage, low_stage, high_stage,
    load_sem, store_sem, rows_send, rows_recv, side_send, side_recv,
    field_send, field_recv, swap_sem,
):
    n_comp, n_band = lax.axis_size("comp"), lax.axis_size("band")
    level, band = lax.axis_index("comp"), lax.axis_index("band")
    core = lax.rem(band, 2)
    beside = level + 1 - 2 * lax.rem(level, 2)
    sibling = band + 1 - 2 * core
    has_low, has_high = band > 0, band < n_band - 1
    outer = lax.rem(band + n_band - 1 + 2 * core, n_band)
    has_outer = jnp.logical_and(band > 0, band < n_band - 1)
    slots = masses.shape[0]

    def load(t):
        return pltpu.make_async_copy(mass_ref.at[t], masses.at[t], load_sem.at[t])

    def store(t):
        return pltpu.make_async_copy(masses.at[t], out_ref.at[t], store_sem.at[t])

    def down(t):
        return pltpu.make_async_remote_copy(
            src_ref=mass_ref.at[t, :, pl.ds(0, HALO), :],
            dst_ref=highs.at[t],
            send_sem=rows_send.at[0, t],
            recv_sem=rows_recv.at[0, t],
            device_id={"band": lax.max(band - 1, 0)},
            device_id_type=MESH_ID,
        )

    def up(t):
        return pltpu.make_async_remote_copy(
            src_ref=mass_ref.at[t, :, pl.ds(HALO, HALO), :],
            dst_ref=lows.at[t],
            send_sem=rows_send.at[1, t],
            recv_sem=rows_recv.at[1, t],
            device_id={"band": lax.min(band + 1, n_band - 1)},
            device_id_type=MESH_ID,
        )

    def send_rows(first, last):
        @pl.when(has_low)
        def _():
            @pl.loop(first, last)
            def _(t):
                down(t).start()

        @pl.when(has_high)
        def _():
            @pl.loop(first, last)
            def _(t):
                up(t).start()

    barrier = pltpu.get_barrier_semaphore()
    peers = [{"comp": beside}, {"band": sibling}]
    peers += [{"comp": lax.rem(level + 2 * p, n_comp)} for p in range(1, n_comp // 2)]
    for peer in peers:
        pl.semaphore_signal(barrier, inc=1, device_id=peer, device_id_type=MESH_ID)

    @pl.when(has_outer)
    def _():
        pl.semaphore_signal(barrier, inc=1, device_id={"band": outer}, device_id_type=MESH_ID)

    @pl.loop(0, slots)
    def _(t):
        load(t).start()

    own = jnp.concatenate([h_ref[...], u_ref[...], v_ref[...]], axis=0)
    own = permuted(own, deal_ref[...])
    for f in range(3):
        fields[level, f, HALO : HALO + ROWS, :] = own[f * ROWS : (f + 1) * ROWS]

    edge = pl.multiple_of(2 * (HALO + HALO // 2) * core, HALO)

    @pl.when(jnp.logical_not(has_outer))
    def _():
        fields[level, :, pl.ds(edge, HALO), :] = jnp.zeros((3, HALO, NX), jnp.float32)

    @pl.when(jnp.logical_not(has_low))
    def _():
        lows[...] = jnp.zeros_like(lows)

    @pl.when(jnp.logical_not(has_high))
    def _():
        highs[...] = jnp.zeros_like(highs)

    pl.semaphore_wait(barrier, len(peers) + has_outer.astype(jnp.int32))

    side = pltpu.make_async_remote_copy(
        src_ref=fields.at[level, :, pl.ds(pl.multiple_of(HALO + HALO * core, HALO), HALO), :],
        dst_ref=fields.at[level, :, pl.ds(pl.multiple_of(3 * HALO * (1 - core), HALO), HALO), :],
        send_sem=side_send,
        recv_sem=side_recv,
        device_id={"band": outer},
        device_id_type=MESH_ID,
    )

    @pl.when(has_outer)
    def _():
        side.start()

    def piece(k, owner, target, lane):
        rows = pl.ds(HALO, ROWS) if k == 0 else pl.ds(edge, HALO)
        return pltpu.make_async_remote_copy(
            src_ref=fields.at[owner, :, rows, :],
            dst_ref=fields.at[owner, :, rows, :],
            send_sem=field_send.at[k, lane],
            recv_sem=field_recv.at[k, lane],
            device_id={"comp": target},
            device_id_type=MESH_ID,
        )

    ring = range(1, n_comp // 2)

    def to_all(k):
        sends = [piece(k, level, beside, 0)]
        sends += [piece(k, level, lax.rem(level + 2 * p, n_comp), p) for p in ring]
        return sends

    def passed_on(k):
        return [piece(k, beside, lax.rem(level + 2 * p, n_comp), n_comp // 2 + p) for p in ring]

    def arriving(k):
        far = [lax.rem(level + n_comp - 2 * p, n_comp) for p in ring]
        waits = [piece(k, owner, beside, p) for p, owner in zip(ring, far)]
        far = [lax.rem(beside + n_comp - 2 * p, n_comp) for p in ring]
        return waits + [piece(k, owner, beside, n_comp // 2 + p) for p, owner in zip(ring, far)]

    for send in to_all(0):
        send.start()
    send_rows(0, EARLY)

    @pl.when(has_outer)
    def _():
        side.wait_recv()

    for send in to_all(1):
        send.start()
    for k in range(2):
        piece(k, beside, beside, 0).wait_recv()
        for send in passed_on(k):
            send.start()
    for wait in arriving(0):
        wait.wait_recv()

    swap = pltpu.make_async_remote_copy(
        src_ref=fields.at[:, :, pl.ds(pl.multiple_of(2 * HALO - HALO * core, HALO), HALO), :],
        dst_ref=fields.at[:, :, pl.ds(pl.multiple_of(3 * HALO * core, HALO), HALO), :],
        send_sem=swap_sem.at[0],
        recv_sem=swap_sem.at[1],
        device_id={"band": sibling},
        device_id_type=MESH_ID,
    )
    swap.start()
    for wait in arriving(1):
        wait.wait_recv()
    send_rows(EARLY, slots)
    swap.wait_recv()

    dynamics(
        fields, back_ref, inv_ref, east_ref, south_ref, (h_out, u_out, v_out),
        h_buf, u_buf, v_buf, g_stage, picked_ref,
    )

    @pl.loop(0, slots)
    def _(t):
        load(t).wait()

        @pl.when(has_low)
        def _():
            up(t).wait_recv()

        @pl.when(has_high)
        def _():
            down(t).wait_recv()

        sides = (LEVELS * HALO, NX)
        blocks = (
            (masses[t].reshape(LEVELS * ROWS, NX), stage),
            (lows[t].reshape(sides), low_stage),
            (highs[t].reshape(sides), high_stage),
        )
        for block, to in blocks:
            dealt = permuted(block, deal_ref[...])
            for i in range(TILES):
                to[i] = dealt[:, columns(i)]
        for j in range(HALO):
            buf[j] = level_rows(low_stage, j, HALO)
            buf[HALO + ROWS + j] = level_rows(high_stage, j, HALO)
        for j in range(ROWS):
            buf[HALO + j] = level_rows(stage, j, ROWS)
        advance_slot(table_ref[1 + t] > 0, buf, stage, inv_ref, east_ref, south_ref)
        final = jnp.concatenate([stage[i] for i in range(TILES)], axis=1)
        final = permuted(final, back_ref[...])
        final = jnp.where(t < table_ref[0], final, 0.0)
        masses[t] = final.reshape(LEVELS, ROWS, NX)
        store(t).start()

    @pl.loop(0, slots)
    def _(t):
        store(t).wait()

        @pl.when(has_low)
        def _():
            down(t).wait_send()

        @pl.when(has_high)
        def _():
            up(t).wait_send()

    @pl.when(has_outer)
    def _():
        side.wait_send()

    swap.wait_send()
    for k in range(2):
        for send in to_all(k) + passed_on(k):
            send.wait_send()


def on_device(tracer_mass, layer_mass, zonal_wind, merid_wind, group_counts, limiter_flags):
    n_comp = lax.axis_size("comp")
    comp = lax.axis_index("comp")
    slots = tracer_mass.shape[0]

    groups = lax.broadcasted_iota(jnp.int32, (n_comp,), 0)
    count = jnp.sum(jnp.where(groups == comp, group_counts, 0))
    start = jnp.sum(jnp.where(groups < comp, group_counts, 0))
    numbers = lax.broadcasted_iota(jnp.int32, (slots, limiter_flags.shape[0]), 1)
    wanted = start + lax.broadcasted_iota(jnp.int32, (slots, limiter_flags.shape[0]), 0)
    flags = jnp.sum(jnp.where(numbers == wanted, limiter_flags[None, :], 0), 1)
    table = jnp.concatenate([count[None], flags])

    deal = dealing()
    f32 = jnp.float32
    vmem = pl.BlockSpec(memory_space=pltpu.VMEM)
    hbm = pl.BlockSpec(memory_space=pl.ANY)
    field = jax.ShapeDtypeStruct((ROWS, NX), f32)
    rows = pltpu.VMEM((STEPS, EXT, LEVELS, NX), f32)
    sides = pltpu.VMEM((slots, LEVELS, HALO, NX), f32)
    state = pltpu.VMEM((EXT, LEVELS, NX), f32)
    dma = pltpu.SemaphoreType.DMA
    out, *fields = pl.pallas_call(
        kernel,
        out_shape=(jax.ShapeDtypeStruct(tracer_mass.shape, f32), field, field, field),
        in_specs=[pl.BlockSpec(memory_space=pltpu.SMEM)] + [vmem] * 5 + [hbm],
        out_specs=(hbm, vmem, vmem, vmem),
        scratch_shapes=[
            pltpu.VMEM((n_comp, 3, EXT, NX), f32),
            pltpu.VMEM(tracer_mass.shape, f32),
            sides,
            sides,
            rows,
            rows,
            rows,
            state,
            state,
            state,
            pltpu.VMEM((TILES, LEVELS * 3 * EXT, 128), f32),
            pltpu.VMEM((3 * ROWS, NX), f32),
            state,
            pltpu.VMEM((TILES, LEVELS * ROWS, 128), f32),
            pltpu.VMEM((TILES, LEVELS * HALO, 128), f32),
            pltpu.VMEM((TILES, LEVELS * HALO, 128), f32),
            dma((slots,)),
            dma((slots,)),
            dma((2, slots)),
            dma((2, slots)),
            dma,
            dma,
            dma((2, n_comp)),
            dma((2, n_comp)),
            dma((2,)),
        ],
        compiler_params=pltpu.CompilerParams(
            collective_id=0, has_side_effects=True, vmem_limit_bytes=VMEM_LIMIT
        ),
    )(
        table,
        layer_mass.reshape(ROWS, NX),
        zonal_wind.reshape(ROWS, NX),
        merid_wind.reshape(ROWS, NX),
        deal,
        deal.T,
        tracer_mass,
    )
    return (out, *(field[None] for field in fields))


def solution(mesh):
    placed = (
        P("comp", None, "band", None),
        P("comp", "band", None),
        P("comp", "band", None),
        P("comp", "band", None),
        P(),
        P(),
    )
    return jax.shard_map(
        on_device,
        mesh=mesh,
        in_specs=placed,
        out_specs=placed[:4],
        check_vma=False,
    )
```

time: 145 us -> 110 us (0.76)
  the two profiles are of different devices: /device:TPU:91 before, /device:TPU:1 now
where the time goes in v2:
time: 110 us; the launch traced here: 108 us
  Pallas kernels  92.5 us (84%)
  local copies, waits for them, and re-layouts  11 us (10%)
  other arithmetic  4.23 us (4%)
    pallas_call x1, Pallas kernels, on_device(): pl.pallas_call(kernel, out_shape=(jax.ShapeDtypeStruct(tracer_mass.shape,...  92.5 us
    unnamed x10, local copies, waits for them, and re-layouts  11 us

profile of v2, /device:TPU:1, one launch (start us, length us, event | category | flops | bytes accessed | tf_op | source)
XLA Modules:
  0.0 108.4 jit_solution(17735499681468636790)
XLA Ops:
  0.6 1.3 %fusion.8 = (s32[]{:T(128)}, s32[]{:T(128)}) fusion(s32[8]{0:T(128)} %param.10, s32[]{:T(128)S(6)} %axis_index.12), kind=kLoop, calls=%fused_computation.18 | loop fusion | flops 46 | bytes 44 | tf_op jit(solution)/shard_map/reduce_sum | solution.py:412
  1.9 0.6 iota_add_fusion
  2.6 0.8 select_reduce_fusion
  3.4 0.7 pad_add_fusion.table_ref
  4.2 0.7 fusion.1
  4.9 0.0 copy-start
  4.9 0.7 copy-done
  5.7 0.0 copy-start.1
  5.7 0.8 copy-done.1
  6.4 0.0 copy-start.2
  6.4 0.8 copy-done.2
  7.2 92.5 %shard_map.93 = (f32[24,8,16,512]{3,2,1,0:T(8,128)}, f32[16,512]{1,0:T(8,128)S(1)}, f32[16,512]{1,0:T(8,128)S(1)}, f32[16,512]{1,0:T(8,128)S(1)}) custom-call(s32[25]{0:T(128)S(1)} %pad_add_fusion.table_ref, f32[16,512]{1,0:T(8,128)S(1)} %bitcast.7, f32[16,512]{1,0:T(8,128)S(1)} %bitcast.8, f32[16,512]{1,0:T(8,128)S(1)} %bitcast.9, ...), custom_call_target="tpu_custom_call" | custom-call | tf_op jit(solution)/shard_map/pallas_call | solution.py:428
  99.7 6.9 %copy.14 = f32[24,8,16,512]{3,2,1,0:T(8,128)} copy(f32[24,8,16,512]{3,2,1,0:T(8,128)} %get-tuple-element.26) | data formatting | bytes 12582912
  106.6 0.6 copy.15
  107.2 0.6 copy.16
  107.8 0.6 copy.17
  (3 shorter events, 0.0 us)
Async XLA Ops:
  4.9 0.8 copy-start
  5.7 0.8 copy-start.1
  6.4 0.8 copy-start.2

commit v3 on v2

--- a/solution.py
+++ b/solution.py
@@ -1,5 +1,6 @@
 import jax
 import jax.numpy as jnp
+import numpy as np
 from jax import lax
 from jax.experimental import pallas as pl
 from jax.experimental.pallas import tpu as pltpu
@@ -13,10 +14,10 @@
 NX = 512
 SLOTS = 24
 BLOCK = 4
-EARLY = 4
+EARLY = 5
 TILES = NX // 128
 MESH_ID = pl.DeviceIdType.MESH
-VMEM_LIMIT = 48 * 1024 * 1024
+VMEM_LIMIT = 40 * 1024 * 1024
 
 time_step = 0.1
 gravity = 0.25
@@ -56,10 +57,9 @@
 
 
 def dealing():
-    source = lax.broadcasted_iota(jnp.int32, (NX, NX), 0)
-    place = lax.broadcasted_iota(jnp.int32, (NX, NX), 1)
-    deal = source == (place % 128) * (NX // 128) + place // 128
-    return deal.astype(jnp.bfloat16)
+    place = np.arange(NX)
+    source = (place % 128) * (NX // 128) + place // 128
+    return (np.arange(NX)[:, None] == source[None, :]).astype(jnp.bfloat16)
 
 
 def permuted(value, table):
@@ -180,11 +180,11 @@
 
 
 def kernel(
-    table_ref, h_ref, u_ref, v_ref, deal_ref, back_ref, mass_ref,
+    counts_ref, flags_ref, h_ref, u_ref, v_ref, deal_ref, back_ref, mass_ref,
     out_ref, h_out, u_out, v_out,
     fields, masses, lows, highs, inv_ref, east_ref, south_ref,
-    h_buf, u_buf, v_buf, g_stage, picked_ref, buf, stage, low_stage, high_stage,
-    load_sem, store_sem, rows_send, rows_recv, side_send, side_recv,
+    h_buf, u_buf, v_buf, g_stage, picked_ref, buf, dealt, stage, low_stage, high_stage,
+    load_sem, rows_send, rows_recv, side_send, side_recv,
     field_send, field_recv, swap_sem,
 ):
     n_comp, n_band = lax.axis_size("comp"), lax.axis_size("band")
@@ -197,11 +197,13 @@
     has_outer = jnp.logical_and(band > 0, band < n_band - 1)
     slots = masses.shape[0]
 
+    count, start = counts_ref[level], 0
+    for g in range(n_comp):
+        start = start + jnp.where(g < level, counts_ref[g], 0)
+    last_flag = flags_ref.shape[0] - 1
+
     def load(t):
         return pltpu.make_async_copy(mass_ref.at[t], masses.at[t], load_sem.at[t])
-
-    def store(t):
-        return pltpu.make_async_copy(masses.at[t], out_ref.at[t], store_sem.at[t])
 
     def down(t):
         return pltpu.make_async_remote_copy(
@@ -311,9 +313,17 @@
         far = [lax.rem(beside + n_comp - 2 * p, n_comp) for p in ring]
         return waits + [piece(k, owner, beside, n_comp // 2 + p) for p, owner in zip(ring, far)]
 
+    def deal_slots(first, last):
+        @pl.loop(first, last)
+        def _(t):
+            load(t).wait()
+            block = permuted(masses[t].reshape(LEVELS * ROWS, NX), deal_ref[...])
+            for i in range(TILES):
+                dealt[t, i] = block[:, columns(i)]
+
     for send in to_all(0):
         send.start()
-    send_rows(0, EARLY)
+    deal_slots(0, 4)
 
     @pl.when(has_outer)
     def _():
@@ -325,6 +335,8 @@
         piece(k, beside, beside, 0).wait_recv()
         for send in passed_on(k):
             send.start()
+    send_rows(0, EARLY)
+    deal_slots(4, slots)
     for wait in arriving(0):
         wait.wait_recv()
 
@@ -337,9 +349,9 @@
         device_id_type=MESH_ID,
     )
     swap.start()
+    send_rows(EARLY, slots)
     for wait in arriving(1):
         wait.wait_recv()
-    send_rows(EARLY, slots)
     swap.wait_recv()
 
     dynamics(
@@ -349,8 +361,6 @@
 
     @pl.loop(0, slots)
     def _(t):
-        load(t).wait()
-
         @pl.when(has_low)
         def _():
             up(t).wait_recv()
@@ -361,30 +371,27 @@
 
         sides = (LEVELS * HALO, NX)
         blocks = (
-            (masses[t].reshape(LEVELS * ROWS, NX), stage),
             (lows[t].reshape(sides), low_stage),
             (highs[t].reshape(sides), high_stage),
         )
         for block, to in blocks:
-            dealt = permuted(block, deal_ref[...])
+            moved = permuted(block, deal_ref[...])
             for i in range(TILES):
-                to[i] = dealt[:, columns(i)]
+                to[i] = moved[:, columns(i)]
         for j in range(HALO):
             buf[j] = level_rows(low_stage, j, HALO)
             buf[HALO + ROWS + j] = level_rows(high_stage, j, HALO)
         for j in range(ROWS):
-            buf[HALO + j] = level_rows(stage, j, ROWS)
-        advance_slot(table_ref[1 + t] > 0, buf, stage, inv_ref, east_ref, south_ref)
+            buf[HALO + j] = level_rows(dealt.at[t], j, ROWS)
+        limited = flags_ref[jnp.minimum(start + t, last_flag)] > 0
+        advance_slot(limited, buf, stage, inv_ref, east_ref, south_ref)
         final = jnp.concatenate([stage[i] for i in range(TILES)], axis=1)
         final = permuted(final, back_ref[...])
-        final = jnp.where(t < table_ref[0], final, 0.0)
-        masses[t] = final.reshape(LEVELS, ROWS, NX)
-        store(t).start()
+        final = jnp.where(t < count, final, 0.0)
+        out_ref[t] = final.reshape(LEVELS, ROWS, NX)
 
     @pl.loop(0, slots)
     def _(t):
-        store(t).wait()
-
         @pl.when(has_low)
         def _():
             down(t).wait_send()
@@ -405,16 +412,7 @@
 
 def on_device(tracer_mass, layer_mass, zonal_wind, merid_wind, group_counts, limiter_flags):
     n_comp = lax.axis_size("comp")
-    comp = lax.axis_index("comp")
     slots = tracer_mass.shape[0]
-
-    groups = lax.broadcasted_iota(jnp.int32, (n_comp,), 0)
-    count = jnp.sum(jnp.where(groups == comp, group_counts, 0))
-    start = jnp.sum(jnp.where(groups < comp, group_counts, 0))
-    numbers = lax.broadcasted_iota(jnp.int32, (slots, limiter_flags.shape[0]), 1)
-    wanted = start + lax.broadcasted_iota(jnp.int32, (slots, limiter_flags.shape[0]), 0)
-    flags = jnp.sum(jnp.where(numbers == wanted, limiter_flags[None, :], 0), 1)
-    table = jnp.concatenate([count[None], flags])
 
     deal = dealing()
     f32 = jnp.float32
@@ -428,8 +426,8 @@
     out, *fields = pl.pallas_call(
         kernel,
         out_shape=(jax.ShapeDtypeStruct(tracer_mass.shape, f32), field, field, field),
-        in_specs=[pl.BlockSpec(memory_space=pltpu.SMEM)] + [vmem] * 5 + [hbm],
-        out_specs=(hbm, vmem, vmem, vmem),
+        in_specs=[pl.BlockSpec(memory_space=pltpu.SMEM)] * 2 + [vmem] * 5 + [hbm],
+        out_specs=(vmem, vmem, vmem, vmem),
         scratch_shapes=[
             pltpu.VMEM((n_comp, 3, EXT, NX), f32),
             pltpu.VMEM(tracer_mass.shape, f32),
@@ -444,10 +442,10 @@
             pltpu.VMEM((TILES, LEVELS * 3 * EXT, 128), f32),
             pltpu.VMEM((3 * ROWS, NX), f32),
             state,
+            pltpu.VMEM((slots, TILES, LEVELS * ROWS, 128), f32),
             pltpu.VMEM((TILES, LEVELS * ROWS, 128), f32),
             pltpu.VMEM((TILES, LEVELS * HALO, 128), f32),
             pltpu.VMEM((TILES, LEVELS * HALO, 128), f32),
-            dma((slots,)),
             dma((slots,)),
             dma((2, slots)),
             dma((2, slots)),
@@ -461,12 +459,13 @@
             collective_id=0, has_side_effects=True, vmem_limit_bytes=VMEM_LIMIT
         ),
     )(
-        table,
+        group_counts,
+        limiter_flags,
         layer_mass.reshape(ROWS, NX),
         zonal_wind.reshape(ROWS, NX),
         merid_wind.reshape(ROWS, NX),
-        deal,
-        deal.T,
+        jnp.asarray(deal),
+        jnp.asarray(deal.T),
         tracer_mass,
     )
     return (out, *(field[None] for field in fields))

time: 110 us -> 99.4 us (0.904)
  Pallas kernels: 92.5 us -> 84.2 us
  other arithmetic: 4.23 us -> 0 us
  local copies, waits for them, and re-layouts: 11 us -> 13 us
    pallas_call x1, Pallas kernels: 92.5 us -> 84.2 us  [on_device(): pl.pallas_call(kernel, out_shape=(jax.ShapeDtypeStruct(tracer_mass.shape,...]
    reduce_sum x2 -> x0, other arithmetic: 2.13 us -> none  [the longest x1 1.3 us: on_device(): count = jnp.sum(jnp.where(groups == comp, group_counts, 0))]
    unnamed x10 -> x20, local copies, waits for them, and re-layouts: 11 us -> 13 us
where the time goes in v3:
time: 99.4 us; the launch traced here: 97.9 us
  Pallas kernels  84.2 us (85%)
  local copies, waits for them, and re-layouts  13 us (13%)
    pallas_call x1, Pallas kernels, on_device(): pl.pallas_call(kernel, out_shape=(jax.ShapeDtypeStruct(tracer_mass.shape,...  84.2 us
    unnamed x20, local copies, waits for them, and re-layouts  13 us

profile of v3, /device:TPU:1, one launch (start us, length us, event | category | flops | bytes accessed | tf_op | source)
XLA Modules:
  0.0 97.9 jit_solution(15390879248750076753)
XLA Ops:
  0.6 0.0 copy-start
  0.6 2.8 %copy-done = f32[24,8,16,512]{3,2,1,0:T(8,128)S(1)} copy-done((f32[24,8,16,512]{3,2,1,0:T(8,128)S(1)}, f32[24,8,16,512]{3,2,1,0:T(8,128)}, u32[]{:S(2)}) %copy-start) | copy-done | bytes 6291480
  3.4 0.0 copy-start.1
  3.4 1.0 %copy-done.1 = bf16[512,512]{1,0:T(8,128)(2,1)S(1)} copy-done((bf16[512,512]{1,0:T(8,128)(2,1)S(1)}, bf16[512,512]{1,0:T(8,128)(2,1)}, u32[]{:S(2)}) %copy-start.1) | copy-done | bytes 524312
  4.5 0.0 copy-start.2
  4.5 1.0 %copy-done.2 = bf16[512,512]{1,0:T(8,128)(2,1)S(1)} copy-done((bf16[512,512]{1,0:T(8,128)(2,1)S(1)}, bf16[512,512]{1,0:T(8,128)(2,1)}, u32[]{:S(2)}) %copy-start.2) | copy-done | bytes 524312
  5.5 0.0 copy-start.3
  5.5 0.8 copy-done.3
  6.3 0.0 copy-start.4
  6.3 0.8 copy-done.4
  7.0 0.0 copy-start.5
  7.0 0.8 copy-done.5
  7.8 0.0 copy-start.6
  7.8 0.7 copy-done.6
  8.4 0.0 copy-start.7
  8.4 0.7 copy-done.7
  9.1 84.2 %shard_map.111 = (f32[24,8,16,512]{3,2,1,0:T(8,128)S(1)}, f32[16,512]{1,0:T(8,128)S(1)}, f32[16,512]{1,0:T(8,128)S(1)}, f32[16,512]{1,0:T(8,128)S(1)}) custom-call(s32[8]{0:T(128)S(1)} %copy-done.6, s32[96]{0:T(128)S(1)} %copy-done.7, f32[16,512]{1,0:T(8,128)S(1)} %bitcast.6, f32[16,512]{1,0:T(8,128)S(1)} %bitcast.7, f32[16,512]{1,0:T(8,128)S(1)} %bitcast.8, ...), custom_call_target="tpu_custom_call" | custom-call | tf_op jit(solution)/shard_map/pallas_call | solution.py:426
  93.3 2.7 %copy.16 = f32[24,8,16,512]{3,2,1,0:T(8,128)} copy(f32[24,8,16,512]{3,2,1,0:T(8,128)S(1)} %get-tuple-element.16) | data formatting | bytes 12582912
  96.0 0.6 copy.17
  96.6 0.6 copy.18
  97.3 0.6 copy.19
Async XLA Ops:
  0.6 2.8 %copy-start = (f32[24,8,16,512]{3,2,1,0:T(8,128)S(1)}, f32[24,8,16,512]{3,2,1,0:T(8,128)}, u32[]{:S(2)}) copy-start(f32[24,8,16,512]{3,2,1,0:T(8,128)} %mass_ref.1) | copy-start | bytes 18874372
  3.4 1.0 %copy-start.1 = (bf16[512,512]{1,0:T(8,128)(2,1)S(1)}, bf16[512,512]{1,0:T(8,128)(2,1)}, u32[]{:S(2)}) copy-start(bf16[512,512]{1,0:T(8,128)(2,1)} %constant.5.clone.back_ref) | copy-start | bytes 1572868
  4.5 1.0 %copy-start.2 = (bf16[512,512]{1,0:T(8,128)(2,1)S(1)}, bf16[512,512]{1,0:T(8,128)(2,1)}, u32[]{:S(2)}) copy-start(bf16[512,512]{1,0:T(8,128)(2,1)} %constant.4.clone.deal_ref) | copy-start | bytes 1572868
  5.5 0.8 copy-start.3
  6.3 0.8 copy-start.4
  7.0 0.8 copy-start.5
  7.8 0.7 copy-start.6
  8.4 0.7 copy-start.7

commit v4 on v3

--- a/solution.py
+++ b/solution.py
@@ -1,6 +1,5 @@
 import jax
 import jax.numpy as jnp
-import numpy as np
 from jax import lax
 from jax.experimental import pallas as pl
 from jax.experimental.pallas import tpu as pltpu
@@ -17,7 +16,7 @@
 EARLY = 5
 TILES = NX // 128
 MESH_ID = pl.DeviceIdType.MESH
-VMEM_LIMIT = 40 * 1024 * 1024
+VMEM_LIMIT = 45 * 1024 * 1024
 
 time_step = 0.1
 gravity = 0.25
@@ -56,10 +55,18 @@
     return jnp.concatenate(made, axis=-1)
 
 
-def dealing():
-    place = np.arange(NX)
-    source = (place % 128) * (NX // 128) + place // 128
-    return (np.arange(NX)[:, None] == source[None, :]).astype(jnp.bfloat16)
+def make_dealing(table_ref, backward):
+    chunk = 32
+
+    @pl.loop(0, NX // chunk)
+    def _(c):
+        source = lax.broadcasted_iota(jnp.int32, (chunk, NX), 0) + c * chunk
+        place = lax.broadcasted_iota(jnp.int32, (chunk, NX), 1)
+        if backward:
+            source, place = place, source
+        dealt = (place & 127) * TILES + (place >> 7) == source
+        rows = pl.ds(pl.multiple_of(c * chunk, chunk), chunk)
+        table_ref[rows, :] = jnp.where(dealt, 1.0, 0.0).astype(jnp.bfloat16)
 
 
 def permuted(value, table):
@@ -73,7 +80,7 @@
     return total
 
 
-def dynamics(fields, back_ref, inv_ref, east_ref, south_ref, last_refs, h_buf, u_buf, v_buf, stage, picked_ref):
+def dynamics(fields, back_ref, inv_ref, east_ref, south_ref, last_ref, h_buf, u_buf, v_buf, stage, picked_ref):
     level, band = lax.axis_index("comp"), lax.axis_index("band")
     first_row, total_rows = band * ROWS, lax.axis_size("band") * ROWS
     stride = 3 * EXT
@@ -137,9 +144,7 @@
         for j in range(ROWS):
             picked = jnp.where(own, buf[HALO + j], 0.0)
             picked_ref[pl.ds(f * ROWS + j, 1), :] = jnp.sum(picked, axis=0, keepdims=True)
-    last = permuted(picked_ref[...], back_ref[...])
-    for f in range(3):
-        last_refs[f][...] = last[f * ROWS : (f + 1) * ROWS]
+    last_ref[...] = permuted(picked_ref[...], back_ref[...])
 
 
 def advance_slot(limited, buf, stage, inv_ref, east_ref, south_ref):
@@ -180,12 +185,12 @@
 
 
 def kernel(
-    counts_ref, flags_ref, h_ref, u_ref, v_ref, deal_ref, back_ref, mass_ref,
-    out_ref, h_out, u_out, v_out,
-    fields, masses, lows, highs, inv_ref, east_ref, south_ref,
+    counts_ref, flags_ref, h_ref, u_ref, v_ref, mass_ref,
+    out_ref, last_ref,
+    own_ref, deal_ref, back_ref, fields, masses, lows, highs, inv_ref, east_ref, south_ref,
     h_buf, u_buf, v_buf, g_stage, picked_ref, buf, dealt, stage, low_stage, high_stage,
     load_sem, rows_send, rows_recv, side_send, side_recv,
-    field_send, field_recv, swap_sem,
+    field_send, field_recv, swap_sem, first_sem,
 ):
     n_comp, n_band = lax.axis_size("comp"), lax.axis_size("band")
     level, band = lax.axis_index("comp"), lax.axis_index("band")
@@ -238,6 +243,15 @@
             def _(t):
                 up(t).start()
 
+    firsts = []
+    for f, ref in enumerate((h_ref, u_ref, v_ref)):
+        firsts.append((ref, own_ref.at[pl.ds(f * ROWS, ROWS), :]))
+    firsts = [
+        pltpu.make_async_copy(src, dst, first_sem.at[n]) for n, (src, dst) in enumerate(firsts)
+    ]
+    for first in firsts:
+        first.start()
+
     barrier = pltpu.get_barrier_semaphore()
     peers = [{"comp": beside}, {"band": sibling}]
     peers += [{"comp": lax.rem(level + 2 * p, n_comp)} for p in range(1, n_comp // 2)]
@@ -252,8 +266,10 @@
     def _(t):
         load(t).start()
 
-    own = jnp.concatenate([h_ref[...], u_ref[...], v_ref[...]], axis=0)
-    own = permuted(own, deal_ref[...])
+    make_dealing(deal_ref, False)
+    for first in firsts:
+        first.wait()
+    own = permuted(own_ref[...], deal_ref[...])
     for f in range(3):
         fields[level, f, HALO : HALO + ROWS, :] = own[f * ROWS : (f + 1) * ROWS]
 
@@ -323,7 +339,7 @@
 
     for send in to_all(0):
         send.start()
-    deal_slots(0, 4)
+    make_dealing(back_ref, True)
 
     @pl.when(has_outer)
     def _():
@@ -336,7 +352,7 @@
         for send in passed_on(k):
             send.start()
     send_rows(0, EARLY)
-    deal_slots(4, slots)
+    deal_slots(0, slots)
     for wait in arriving(0):
         wait.wait_recv()
 
@@ -355,7 +371,7 @@
     swap.wait_recv()
 
     dynamics(
-        fields, back_ref, inv_ref, east_ref, south_ref, (h_out, u_out, v_out),
+        fields, back_ref, inv_ref, east_ref, south_ref, last_ref,
         h_buf, u_buf, v_buf, g_stage, picked_ref,
     )
 
@@ -414,21 +430,25 @@
     n_comp = lax.axis_size("comp")
     slots = tracer_mass.shape[0]
 
-    deal = dealing()
     f32 = jnp.float32
     vmem = pl.BlockSpec(memory_space=pltpu.VMEM)
     hbm = pl.BlockSpec(memory_space=pl.ANY)
-    field = jax.ShapeDtypeStruct((ROWS, NX), f32)
     rows = pltpu.VMEM((STEPS, EXT, LEVELS, NX), f32)
     sides = pltpu.VMEM((slots, LEVELS, HALO, NX), f32)
     state = pltpu.VMEM((EXT, LEVELS, NX), f32)
     dma = pltpu.SemaphoreType.DMA
-    out, *fields = pl.pallas_call(
+    out, last = pl.pallas_call(
         kernel,
-        out_shape=(jax.ShapeDtypeStruct(tracer_mass.shape, f32), field, field, field),
-        in_specs=[pl.BlockSpec(memory_space=pltpu.SMEM)] * 2 + [vmem] * 5 + [hbm],
-        out_specs=(vmem, vmem, vmem, vmem),
+        out_shape=(
+            jax.ShapeDtypeStruct(tracer_mass.shape, f32),
+            jax.ShapeDtypeStruct((3 * ROWS, NX), f32),
+        ),
+        in_specs=[pl.BlockSpec(memory_space=pltpu.SMEM)] * 2 + [hbm] * 4,
+        out_specs=(vmem, vmem),
         scratch_shapes=[
+            pltpu.VMEM((3 * ROWS, NX), f32),
+            pltpu.VMEM((NX, NX), jnp.bfloat16),
+            pltpu.VMEM((NX, NX), jnp.bfloat16),
             pltpu.VMEM((n_comp, 3, EXT, NX), f32),
             pltpu.VMEM(tracer_mass.shape, f32),
             sides,
@@ -454,6 +474,7 @@
             dma((2, n_comp)),
             dma((2, n_comp)),
             dma((2,)),
+            dma((3,)),
         ],
         compiler_params=pltpu.CompilerParams(
             collective_id=0, has_side_effects=True, vmem_limit_bytes=VMEM_LIMIT
@@ -464,11 +485,10 @@
         layer_mass.reshape(ROWS, NX),
         zonal_wind.reshape(ROWS, NX),
         merid_wind.reshape(ROWS, NX),
-        jnp.asarray(deal),
-        jnp.asarray(deal.T),
         tracer_mass,
     )
-    return (out, *(field[None] for field in fields))
+    last = last.reshape(3, 1, ROWS, NX)
+    return out, last[0], last[1], last[2]
 
 
 def solution(mesh):

time: 99.4 us -> 93.5 us (0.941)
  local copies, waits for them, and re-layouts: 13 us -> 6.92 us
    unnamed x20 -> x11, local copies, waits for them, and re-layouts: 13 us -> 6.28 us
where the time goes in v4:
time: 93.5 us; the launch traced here: 92.1 us
  Pallas kernels  84.6 us (90%)
  local copies, waits for them, and re-layouts  6.92 us (7%)
    pallas_call x1, Pallas kernels, on_device(): pl.pallas_call(kernel, out_shape=(jax.ShapeDtypeStruct(tracer_mass.shape,...  84.6 us
    unnamed x11, local copies, waits for them, and re-layouts  6.28 us

profile of v4, /device:TPU:1, one launch (start us, length us, event | category | flops | bytes accessed | tf_op | source)
XLA Modules:
  0.0 92.1 jit_solution(17933809723858542146)
XLA Ops:
  0.6 0.0 copy-start
  0.6 0.7 copy-done
  1.4 0.0 copy-start.1
  1.4 0.8 copy-done.1
  2.1 0.0 copy-start.2
  2.2 0.8 copy-done.2
  2.9 0.0 copy-start.3
  2.9 0.7 copy-done.3
  3.6 0.0 copy-start.4
  3.6 0.7 copy-done.4
  4.2 84.6 %shard_map.93 = (f32[24,8,16,512]{3,2,1,0:T(8,128)S(1)}, f32[48,512]{1,0:T(8,128)S(1)}) custom-call(s32[8]{0:T(128)S(1)} %copy-done.3, s32[96]{0:T(128)S(1)} %copy-done.4, f32[16,512]{1,0:T(8,128)S(1)} %bitcast.9, f32[16,512]{1,0:T(8,128)S(1)} %bitcast.10, f32[16,512]{1,0:T(8,128)S(1)} %bitcast.11, f32[24,8,16,512]{3,2,1,0:T(8,128)} %mass_ref.1), custom_call_target="tpu_custom_call" | custom-call | tf_op jit(solution)/shard_map/pallas_call | solution.py:440
  88.8 0.6 slice_bitcast_fusion
  89.4 2.7 %copy.11 = f32[24,8,16,512]{3,2,1,0:T(8,128)} copy(f32[24,8,16,512]{3,2,1,0:T(8,128)S(1)} %get-tuple-element.15) | data formatting | bytes 12582912
Async XLA Ops:
  0.6 0.8 copy-start
  1.4 0.8 copy-start.1
  2.1 0.8 copy-start.2
  2.9 0.7 copy-start.3
  3.6 0.7 copy-start.4

commit v5 on v4

--- a/solution.py
+++ b/solution.py
@@ -14,6 +14,7 @@
 SLOTS = 24
 BLOCK = 4
 EARLY = 5
+AHEAD = 3
 TILES = NX // 128
 MESH_ID = pl.DeviceIdType.MESH
 VMEM_LIMIT = 45 * 1024 * 1024
@@ -231,16 +232,14 @@
         )
 
     def send_rows(first, last):
-        @pl.when(has_low)
-        def _():
-            @pl.loop(first, last)
-            def _(t):
+        @pl.loop(first, last)
+        def _(t):
+            @pl.when(has_low)
+            def _():
                 down(t).start()
 
-        @pl.when(has_high)
-        def _():
-            @pl.loop(first, last)
-            def _(t):
+            @pl.when(has_high)
+            def _():
                 up(t).start()
 
     firsts = []
@@ -337,6 +336,8 @@
             for i in range(TILES):
                 dealt[t, i] = block[:, columns(i)]
 
+    ahead = AHEAD * (1 - core)
+    send_rows(0, ahead)
     for send in to_all(0):
         send.start()
     make_dealing(back_ref, True)
@@ -351,7 +352,7 @@
         piece(k, beside, beside, 0).wait_recv()
         for send in passed_on(k):
             send.start()
-    send_rows(0, EARLY)
+    send_rows(ahead, EARLY)
     deal_slots(0, slots)
     for wait in arriving(0):
         wait.wait_recv()

time: 93.5 us -> 93.2 us (level); the launches traced: 92.1 us -> 92.9 us
  no operation moved by 1% of the time
where the time goes in v5:
time: 93.2 us; the launch traced here: 92.9 us
  Pallas kernels  85.3 us (92%)
  local copies, waits for them, and re-layouts  6.92 us (7%)
    pallas_call x1, Pallas kernels, on_device(): pl.pallas_call(kernel, out_shape=(jax.ShapeDtypeStruct(tracer_mass.shape,...  85.3 us
    unnamed x11, local copies, waits for them, and re-layouts  6.28 us

profile of v5, /device:TPU:1, one launch (start us, length us, event | category | flops | bytes accessed | tf_op | source)
XLA Modules:
  0.0 92.9 jit_solution(7092768557174515108)
XLA Ops:
  0.6 0.0 copy-start
  0.6 0.7 copy-done
  1.4 0.0 copy-start.1
  1.4 0.8 copy-done.1
  2.1 0.0 copy-start.2
  2.2 0.8 copy-done.2
  2.9 0.0 copy-start.3
  2.9 0.7 copy-done.3
  3.6 0.0 copy-start.4
  3.6 0.7 copy-done.4
  4.2 85.3 %shard_map.93 = (f32[24,8,16,512]{3,2,1,0:T(8,128)S(1)}, f32[48,512]{1,0:T(8,128)S(1)}) custom-call(s32[8]{0:T(128)S(1)} %copy-done.3, s32[96]{0:T(128)S(1)} %copy-done.4, f32[16,512]{1,0:T(8,128)S(1)} %bitcast.9, f32[16,512]{1,0:T(8,128)S(1)} %bitcast.10, f32[16,512]{1,0:T(8,128)S(1)} %bitcast.11, f32[24,8,16,512]{3,2,1,0:T(8,128)} %mass_ref.1), custom_call_target="tpu_custom_call" | custom-call | tf_op jit(solution)/shard_map/pallas_call | solution.py:441
  89.6 0.6 slice_bitcast_fusion
  90.2 2.7 %copy.11 = f32[24,8,16,512]{3,2,1,0:T(8,128)} copy(f32[24,8,16,512]{3,2,1,0:T(8,128)S(1)} %get-tuple-element.15) | data formatting | bytes 12582912
Async XLA Ops:
  0.6 0.8 copy-start
  1.4 0.8 copy-start.1
  2.1 0.8 copy-start.2
  2.9 0.7 copy-start.3
  3.6 0.7 copy-start.4
